TPU v7x, 256 devices: a whole 4x4x8 slice. The times are simulated.
256 devices in a mesh: dp: 256 (over z, y, x, core).
Axes of the slice: x: 4, y: 4, z: 8, core: 2. Of those that a mesh axis runs over, the one named last changes fastest.
Arguments:
- patches: bfloat16 [2048, 256, 1152], P('dp'), may hold values from -6 to 6
- captions: bfloat16 [2048, 1152], P('dp'), may hold values from -60 to 60
- probe_query: bfloat16 [576], replicated, may hold values from -45 to 45
- key_weight: bfloat16 [1152, 576], replicated, may hold values from -0.1875 to 0.1875
- value_weight: bfloat16 [1152, 576], replicated, may hold values from -0.1875 to 0.1875
- out_weight: bfloat16 [576, 1152], replicated, may hold values from -0.25 to 0.25
- logit_scale: float32 [1], replicated, may hold values from 4 to 16
- logit_bias: float32 [1], replicated, may hold values from -2 to 0
Outputs:
- caption_grad: float32 [2048, 1152], P('dp')
- probe_grad: float32 [576], replicated
- key_grad: bfloat16 [1152, 576], replicated
- value_grad: bfloat16 [1152, 576], replicated
- out_grad: bfloat16 [576, 1152], replicated
All inputs are finite; a program needn't handle non-finite values.
Results may differ from a plain program's by a relative error of at most 0.017.
The roundings to bfloat16 on the way count: a program that leaves them out, or rounds other values in their place, can miss the bound.
Values may be sent and summed in bfloat16 or wider, within the bound.
A program may use at most 64 MiB of HBM per device.

v0:
```python
import math

import jax
import jax.numpy as jnp
from jax import lax
from jax.sharding import PartitionSpec as P

D = 1152
HEADS = 8
HEAD_DIM = 72
PATCHES = 256
CYCLE = 2


norm_epsilon = 1e-06


def passed_along(block, axis, distance):
    devices = range(lax.axis_size(axis))
    route = [((i - distance) % len(devices), i) for i in devices]
    return lax.ppermute(block, axis, route)


def normalize(rows):
    length = jnp.sqrt(jnp.sum(rows * rows, axis=-1, keepdims=True) + norm_epsilon)
    return (rows / length, length)


def on_device(
    patches, captions, probe_query, key_weight, value_weight, out_weight, logit_scale, logit_bias
):
    count = patches.shape[0]
    highest = lax.Precision.HIGHEST
    flat = patches.reshape(count * PATCHES, D)
    probe_low = probe_query.reshape(HEADS, HEAD_DIM)
    key_heads = (
        jnp.dot(flat, key_weight, preferred_element_type=jnp.float32)
        .astype(jnp.bfloat16)
        .reshape(count, PATCHES, HEADS, HEAD_DIM)
    )
    value_heads = (
        jnp.dot(flat, value_weight, preferred_element_type=jnp.float32)
        .astype(jnp.bfloat16)
        .reshape(count, PATCHES, HEADS, HEAD_DIM)
    )
    scores = jnp.einsum(
        "iphd,hd->ihp", key_heads, probe_low, preferred_element_type=jnp.float32
    ) / math.sqrt(HEAD_DIM)
    attention = jax.nn.softmax(scores, axis=-1)
    attention_low = attention.astype(jnp.bfloat16)
    pooled = jnp.einsum(
        "ihp,iphd->ihd", attention_low, value_heads, preferred_element_type=jnp.float32
    ).astype(jnp.bfloat16)
    pooled = pooled.reshape(count, HEADS * HEAD_DIM)
    embedding = jnp.dot(pooled, out_weight, preferred_element_type=jnp.float32)
    image_unit, image_length = normalize(embedding)
    own_unit, own_length = normalize(captions.astype(jnp.float32))
    scale = logit_scale[0]
    bias = logit_bias[0]
    identity = jnp.eye(count, dtype=jnp.float32)
    slope = (
        jax.nn.sigmoid(scale * jnp.dot(image_unit, own_unit.T, precision=highest) + bias) - identity
    )
    image_total = scale * jnp.dot(slope, own_unit, precision=highest)
    own_term = scale * jnp.dot(slope.T, image_unit, precision=highest)
    visiting = captions
    visit_terms = []
    for offset in range(1, CYCLE + 1):
        visiting = passed_along(visiting, "dp", 1)
        visit_unit = normalize(visiting.astype(jnp.float32))[0]
        slope = jax.nn.sigmoid(scale * jnp.dot(image_unit, visit_unit.T, precision=highest) + bias)
        image_total = image_total + scale * jnp.dot(slope, visit_unit, precision=highest)
        visit_terms.append(scale * jnp.dot(slope.T, image_unit, precision=highest))
    carried = own_term
    for offset in range(1, CYCLE + 1):
        carried = passed_along(carried, "dp", 1) + visit_terms[offset - 1]
    caption_total = passed_along(carried, "dp", -CYCLE)
    caption_grad = (
        caption_total - own_unit * jnp.sum(own_unit * caption_total, axis=-1, keepdims=True)
    ) / own_length
    embedding_grad = (
        (image_total - image_unit * jnp.sum(image_unit * image_total, axis=-1, keepdims=True))
        / image_length
    ).astype(jnp.bfloat16)
    out_part = jnp.einsum("nk,nd->kd", pooled, embedding_grad, preferred_element_type=jnp.float32)
    pooled_grad = jnp.einsum(
        "nd,kd->nk", embedding_grad, out_weight, preferred_element_type=jnp.float32
    ).reshape(count, HEADS, HEAD_DIM)
    attention_grad = jnp.einsum(
        "ihd,iphd->ihp", pooled_grad, value_heads, preferred_element_type=jnp.float32
    )
    score_grad = attention * (
        attention_grad - jnp.sum(attention * attention_grad, axis=-1, keepdims=True)
    )
    value_rows_grad = (
        jnp.einsum("ihp,ihd->iphd", attention, pooled_grad)
        .astype(jnp.bfloat16)
        .reshape(count * PATCHES, HEADS * HEAD_DIM)
    )
    value_part = jnp.einsum("nc,nk->ck", flat, value_rows_grad, preferred_element_type=jnp.float32)
    score_low = score_grad.astype(jnp.bfloat16)
    patch_part = jnp.einsum("ipc,ihp->ch", patches, score_low, preferred_element_type=jnp.float32)
    probe_part = jnp.einsum(
        "ihp,iphd->hd", score_grad, key_heads, preferred_element_type=jnp.float32
    ) / math.sqrt(HEAD_DIM)
    probe = probe_query.astype(jnp.float32).reshape(HEADS, HEAD_DIM)
    key_part = (patch_part[:, :, None] * probe[None, :, :] / math.sqrt(HEAD_DIM)).reshape(
        D, HEADS * HEAD_DIM
    )
    key_total, value_total, out_total, probe_total = lax.psum(
        (key_part, value_part, out_part, probe_part), "dp"
    )
    return (
        caption_grad,
        probe_total.reshape(HEADS * HEAD_DIM),
        key_total.astype(jnp.bfloat16),
        value_total.astype(jnp.bfloat16),
        out_total.astype(jnp.bfloat16),
    )


def solution(mesh):
    placed = (P("dp", None, None), P("dp", None), P(), P(), P(), P(), P(), P())
    return jax.shard_map(
        on_device,
        mesh=mesh,
        in_specs=placed,
        out_specs=(P("dp", None), P(), P(), P(), P()),
        check_vma=False,
    )
```

profile of v0, /device:TPU:1, one launch (start us, length us, event | category | flops | bytes accessed | tf_op | source)
XLA Modules:
  0.0 203.0 jit_solution(2767527584699683136)
XLA Ops:
  0.6 2.7 %collective-permute-start.1 = (bf16[8,1152]{1,0:T(8,128)(2,1)}, bf16[8,1152]{1,0:T(8,128)(2,1)S(1)}, u32[]{:S(2)}, u32[]{:S(2)}) collective-permute-start(bf16[8,1152]{1,0:T(8,128)(2,1)} %param.9), channel_id=1, source_target_pairs={{255,0},{0,1},{1,2},{2,3},{3,4},{4,5},{5,6},{6,7},{7,8},{8,9},{9,1... | collective-permute-start | bytes 55304 | tf_op jit(solution)/shard_map/ppermute | solution.py:21
  3.3 0.9 fusion.35
  5.5 0.8 reshape.87
  6.3 5.8 %convolution_convert_fusion.1 = bf16[2048,576]{0,1:T(8,128)(2,1)S(1)} fusion(bf16[2048,1152]{1,0:T(8,128)(2,1)} %bitcast.99, bf16[1152,576]{0,1:T(8,128)(2,1)S(1)} %copy-done), kind=kOutput, calls=%fused_computation.4 | convolution fusion | flops 2719088640 | bytes 8404992 | tf_op jit(solution)/shard_map/dot_general | solution.py:37
  12.1 0.8 copy.26
  13.4 1.3 fusion.50
  14.7 0.6 copy-done.3
  15.7 3.5 %convolution_convert_fusion = bf16[2048,576]{0,1:T(8,128)(2,1)S(1)} fusion(bf16[2048,1152]{1,0:T(8,128)(2,1)S(1)} %bitcast.101, bf16[1152,576]{0,1:T(8,128)(2,1)S(1)} %copy-done.8), kind=kOutput, calls=%fused_computation.3 | convolution fusion | flops 2719088640 | bytes 8404992 | tf_op jit(solution)/shard_map/dot_general | solution.py:42
  19.2 0.8 copy.27
  20.1 1.3 copy-done.1
  21.4 0.8 fusion.6
  23.9 1.6 collective-permute-start.3
  27.7 2.6 %fusion.4 = f32[8,8,1,256]{3,2,1,0:T(1,128)S(1)} fusion(f32[8,8,72,1]{2,3,1,0:T(1,128)S(1)} %bitcast.108, bf16[8,256,8,72]{1,0,3,2:T(8,128)(2,1)} %bitcast.97), kind=kOutput, calls=%fused_computation.15 | convolution fusion | flops 2359296 | bytes 2443264 | tf_op jit(solution)/shard_map/ihd,iphd->ihp/dot_general | solution.py:89
  30.5 3.1 %convolution_bitcast_fusion.1 = f32[1152,8]{0,1:T(8,128)S(1)} fusion(bf16[8,256,1152]{2,1,0:T(8,128)(2,1)} %param.8, f32[8,8,256]{2,1,0:T(8,128)S(1)} %get-tuple-element.10, f32[8,8,1,256]{3,2,1,0:T(1,128)S(1)} %fusion.4, f32[8,8]{1,0:T(8,128)S(1)} %fusion.30), kind=kOutput, calls=%fused_computation.14 | convolution fusion | flops 37797888 | bytes 4886784 | tf_op jit(solution)/shard_map/ipc,ihp->ch/dot_general | solution.py:102
  33.6 2.1 %fusion.48 = f32[576,1152]{1,0:T(8,128)} fusion(bf16[8,576]{1,0:T(8,128)(2,1)S(1)} %reshape.73, f32[8,1152]{1,0:T(8,128)S(1)} %get-tuple-element.16, f32[8]{0:T(128)S(1)} %get-tuple-element.15, f32[8]{0:T(128)S(1)} %get-tuple-element.18, f32[8,1152]{1,0:T(8,128)S(1)} %get-tuple-element.14), kind=kOutput, calls=%fused_computation.85 | convolution fusion | flops 10662912 | bytes 2737216 | tf_op jit(solution)/shard_map/nk,nd->kd/dot_general | solution.py:85
  35.7 0.7 fusion.8
  36.8 2.6 %collective-permute-start.2 = (f32[8,1152]{1,0:T(8,128)S(1)}, f32[8,1152]{1,0:T(8,128)S(1)}, u32[]{:S(2)}, u32[]{:S(2)}) collective-permute-start(f32[8,1152]{1,0:T(8,128)S(1)} %fusion.3), channel_id=1, source_target_pairs={{255,0},{0,1},{1,2},{2,3},{3,4},{4,5},{5,6},{6,7},{7,8},{8,9},{9,1... | collective-permute-start | bytes 110600 | tf_op jit(solution)/shard_map/ppermute | solution.py:21
  39.4 0.8 multiply_convert_fusion
  40.1 0.8 copy.28
  40.9 7.1 %convolution_bitcast_fusion = f32[1152,576]{0,1:T(8,128)} fusion(bf16[2048,576]{0,1:T(8,128)(2,1)S(1)} %bitcast.104, bf16[2048,1152]{1,0:T(8,128)(2,1)} %bitcast.100), kind=kOutput, calls=%fused_computation.2 | convolution fusion | flops 2717908992 | bytes 9732096 | tf_op jit(solution)/shard_map/nc,nk->ck/dot_general | solution.py:100
  48.3 12.4 %collective-permute-start.4 = (f32[8,1152]{1,0:T(8,128)S(1)}, f32[8,1152]{1,0:T(8,128)S(1)}, u32[]{:S(2)}, u32[]{:S(2)}) collective-permute-start(f32[8,1152]{1,0:T(8,128)S(1)} %add.87), channel_id=1, source_target_pairs={{2,0},{3,1},{4,2},{5,3},{6,4},{7,5},{8,6},{9,7},{10,8},{11,9},{12,... | collective-permute-start | bytes 110600 | tf_op jit(solution)/shard_map/ppermute | solution.py:21
  60.8 1.8 fusion.1
  62.6 139.5 %all-reduce.2 = (f32[576]{0:T(1024)}, bf16[1152,576]{0,1:T(8,128)(2,1)}, bf16[1152,576]{0,1:T(8,128)(2,1)}, bf16[576,1152]{1,0:T(8,128)(2,1)}) all-reduce(f32[576]{0:T(1024)S(1)} %reshape.75, f32[1152,576]{0,1:T(8,128)} %fusion.1, f32[1152,576]{0,1:T(8,128)} %convolution_bitcast_fusion, ...), channel_id=1, replica_groups=mesh['dp'=256] {'dp'}, use_global_device_ids=true, to_apply=%region_9.0 | all-reduce | flops 1991232 | bytes 11948544 | tf_op jit(solution)/shard_map/psum | solution.py:110
  202.3 0.7 subtract_divide_fusion
  (52 shorter events, 5.9 us)
Async XLA Ops:
  0.6 5.6 %copy-start = (bf16[1152,576]{0,1:T(8,128)(2,1)S(1)}, bf16[1152,576]{0,1:T(8,128)(2,1)}, u32[]{:S(2)}) copy-start(bf16[1152,576]{0,1:T(8,128)(2,1)} %param.11) | copy-start | bytes 3981316
  0.6 23.1 %collective-permute-start.1 = (bf16[8,1152]{1,0:T(8,128)(2,1)}, bf16[8,1152]{1,0:T(8,128)(2,1)S(1)}, u32[]{:S(2)}, u32[]{:S(2)}) collective-permute-start(bf16[8,1152]{1,0:T(8,128)(2,1)} %param.9), channel_id=1, source_target_pairs={{255,0},{0,1},{1,2},{2,3},{3,4},{4,5},{5,6},{6,7},{7,8},{8,9},{9,1... | collective-permute-start | bytes 55304 | tf_op jit(solution)/shard_map/ppermute | solution.py:21
  12.1 3.2 %copy-start.3 = (bf16[8,256,1152]{2,1,0:T(8,128)(2,1)S(1)}, bf16[8,256,1152]{2,1,0:T(8,128)(2,1)}, u32[]{:S(2)}) copy-start(bf16[8,256,1152]{2,1,0:T(8,128)(2,1)} %param.8) | copy-start | bytes 14155780
  12.9 6.3 %copy-start.4 = (bf16[72,8,8,256]{3,2,1,0:T(8,128)(2,1)}, bf16[72,8,8,256]{3,2,1,0:T(8,128)(2,1)S(1)}, u32[]{:S(2)}) copy-start(bf16[72,8,8,256]{3,2,1,0:T(8,128)(2,1)S(1)} %copy.26) | copy-start | bytes 7077892
  12.9 2.8 %copy-start.8 = (bf16[1152,576]{0,1:T(8,128)(2,1)S(1)}, bf16[1152,576]{0,1:T(8,128)(2,1)}, u32[]{:S(2)}) copy-start(bf16[1152,576]{0,1:T(8,128)(2,1)} %param.12) | copy-start | bytes 3981316
  20.0 1.4 copy-start.1
  20.0 2.3 %copy-start.2 = (bf16[576,1152]{1,0:T(8,128)(2,1)S(1)}, bf16[576,1152]{1,0:T(8,128)(2,1)}, u32[]{:S(2)}) copy-start(bf16[576,1152]{1,0:T(8,128)(2,1)} %param.13) | copy-start | bytes 3981316
  20.0 2.7 %copy-start.6 = (bf16[8,1152]{1,0:T(8,128)(2,1)S(1)}, bf16[8,1152]{1,0:T(8,128)(2,1)}, u32[]{:S(2)}) copy-start(bf16[8,1152]{1,0:T(8,128)(2,1)} %param.9) | copy-start | bytes 55300
  21.4 2.2 %copy-start.7 = (bf16[576]{0:T(1024)(128)(2,1)S(1)}, bf16[576]{0:T(1024)(128)(2,1)}, u32[]{:S(2)}) copy-start(bf16[576]{0:T(1024)(128)(2,1)} %param.10) | copy-start | bytes 3460
  23.3 13.3 %collective-permute-start = (f32[8,1152]{1,0:T(8,128)S(1)}, f32[8,1152]{1,0:T(8,128)S(1)}, u32[]{:S(2)}, u32[]{:S(2)}) collective-permute-start(f32[8,1152]{1,0:T(8,128)S(1)} %convolution_multiply_fusion.2), channel_id=1, source_target_pairs={{255,0},{0,1},{1,2},{2,3},{3,4},{4,5},{5,6},{6,7},{7,8},{8,9},{9,1... | collective-permute-start | bytes 110600 | tf_op jit(solution)/shard_map/ppermute | solution.py:21
  23.9 2.5 %collective-permute-start.3 = (bf16[8,1152]{1,0:T(8,128)(2,1)S(1)}, bf16[8,1152]{1,0:T(8,128)(2,1)S(1)}, u32[]{:S(2)}, u32[]{:S(2)}) collective-permute-start(bf16[8,1152]{1,0:T(8,128)(2,1)S(1)} %collective-permute-done.1), channel_id=1, source_target_pairs={{255,0},{0,1},{1,2},{2,3},{3,4},{4,5},{5,6},{6,7},{7,8},{8,9},{9,1... | collective-permute-start | bytes 55304 | tf_op jit(solution)/shard_map/ppermute | solution.py:21
  33.5 2.1 %copy-start.5 = (bf16[72,8,8,256]{3,2,1,0:T(8,128)(2,1)S(1)}, bf16[72,8,8,256]{3,2,1,0:T(8,128)(2,1)}, u32[]{:S(2)}) copy-start(bf16[72,8,8,256]{3,2,1,0:T(8,128)(2,1)} %copy-done.4) | copy-start | bytes 7077892
  36.8 11.4 %collective-permute-start.2 = (f32[8,1152]{1,0:T(8,128)S(1)}, f32[8,1152]{1,0:T(8,128)S(1)}, u32[]{:S(2)}, u32[]{:S(2)}) collective-permute-start(f32[8,1152]{1,0:T(8,128)S(1)} %fusion.3), channel_id=1, source_target_pairs={{255,0},{0,1},{1,2},{2,3},{3,4},{4,5},{5,6},{6,7},{7,8},{8,9},{9,1... | collective-permute-start | bytes 110600 | tf_op jit(solution)/shard_map/ppermute | solution.py:21
  48.3 153.8 %collective-permute-start.4 = (f32[8,1152]{1,0:T(8,128)S(1)}, f32[8,1152]{1,0:T(8,128)S(1)}, u32[]{:S(2)}, u32[]{:S(2)}) collective-permute-start(f32[8,1152]{1,0:T(8,128)S(1)} %add.87), channel_id=1, source_target_pairs={{2,0},{3,1},{4,2},{5,3},{6,4},{7,5},{8,6},{9,7},{10,8},{11,9},{12,... | collective-permute-start | bytes 110600 | tf_op jit(solution)/shard_map/ppermute | solution.py:21
where the time goes:
time: 205 us; the launch traced here: 203 us
  blocking collectives  140 us (68%)
  matrix products  29.4 us (14%)
  starting transfers between devices  19.4 us (9%)
  other arithmetic  6.19 us (3%)
  local copies, waits for them, and re-layouts  5.85 us (3%)
  between operations  2.22 us (1%)
    psum x1, blocking collectives, on_device(): lax.psum((key_part, value_part, out_part, probe_part), 'dp')  140 us
    ppermute x5, starting transfers between devices, passed_along(): return lax.ppermute(block, axis, route)  19.4 us
    dot_general x1, matrix products, on_device(): jnp.einsum('nc,nk->ck', flat, value_rows_grad, preferred_element_type=jnp...  7.07 us
    dot_general x1, matrix products, on_device(): jnp.dot(flat, key_weight, preferred_element_type=jnp.float32)  5.84 us
    unnamed x21, local copies, waits for them, and re-layouts  4.66 us
  transfers between devices with their start and end apart: 5, of which 1 were waited for; matrix products, arithmetic and copies ran while one was open for 19% of the time, Pallas kernels for 0%

commit v1 on v0

--- a/solution.py
+++ b/solution.py
@@ -1,8 +1,11 @@
+import functools
 import math
 
 import jax
 import jax.numpy as jnp
 from jax import lax
+from jax.experimental import pallas as pl
+from jax.experimental.pallas import tpu as pltpu
 from jax.sharding import PartitionSpec as P
 
 D = 1152
@@ -10,6 +13,357 @@
 HEAD_DIM = 72
 PATCHES = 256
 CYCLE = 2
+ROWS = HEADS * HEAD_DIM
+
+MESH = pl.DeviceIdType.MESH
+HALF = 162
+PART = 41
+SLOTS = 21
+OWNED = 3
+GRID = 24
+WIDE = 1280
+
+
+def reduce_kernel(
+    value_ref,
+    rows_ref,
+    small_ref,
+    value_out,
+    out_out,
+    small_out,
+    value_send,
+    value_got,
+    value_own,
+    rows_all,
+    rows_got,
+    small_got,
+    small_pair,
+    small_all,
+    pools,
+    out_own,
+    first_send,
+    first_got,
+    grid,
+    second_got,
+    total,
+    third_got,
+    owned,
+    owned_all,
+    small_owned,
+    small_slots,
+    final,
+    pair_sem,
+    rows_sem,
+    small_sem,
+    first_sem,
+    second_sem,
+    third_sem,
+    back_sem,
+    back_small_sem,
+    spread_sem,
+    spread_small_sem,
+    home_sem,
+    cross_sem,
+):
+    f32, bf16 = jnp.float32, jnp.bfloat16
+    me = lax.axis_index("dp")
+    core, x, y, z = me % 2, (me // 2) % 4, (me // 8) % 4, me // 32
+    first = x + (y - x) * core
+    second = y + (x - y) * core
+
+    def device_at(at_z, at_first, at_second, at_core):
+        at_x = at_first + (at_second - at_first) * core
+        at_y = at_second + (at_first - at_second) * core
+        return ((at_z * 4 + at_y) * 4 + at_x) * 2 + at_core
+
+    other = device_at(z, first, second, 1 - core)
+
+    def first_peer(step):
+        place = (first + step) % 4
+        return device_at(z, place, second, core), place
+
+    def second_peer(step):
+        place = (second + step) % 4
+        return device_at(z, first, place, core), place
+
+    def third_peer(step):
+        place = (z + step) % 8
+        return device_at(place, first, second, core), place
+
+    peers = [other]
+    peers += [first_peer(step)[0] for step in (1, 2, 3)]
+    peers += [second_peer(step)[0] for step in (1, 2, 3)]
+    peers += [third_peer(step)[0] for step in range(1, 8)]
+    barrier = pltpu.get_barrier_semaphore()
+    for peer in peers:
+        pl.semaphore_signal(barrier, inc=1, device_id=(peer,), device_id_type=MESH)
+    pl.semaphore_wait(barrier, len(peers))
+
+    sent = []
+
+    def copy_to(device, source, target, sems, slot):
+        return pltpu.make_async_remote_copy(
+            src_ref=source,
+            dst_ref=target,
+            send_sem=sems.at[0, slot],
+            recv_sem=sems.at[1, slot],
+            device_id=(device,),
+            device_id_type=MESH,
+        )
+
+    def send(*where):
+        copy = copy_to(*where)
+        copy.start()
+        sent.append(copy)
+        return copy
+
+    rows_copy = send(other, rows_ref, rows_got, rows_sem, 0)
+    small_copy = send(other, small_ref, small_got, small_sem, 0)
+
+    away = (1 - core) * 288
+    home = core * 288
+
+    def value_tile(start, row, column):
+        at = pl.multiple_of(start + row * 16, 16)
+        return value_ref[pl.ds(at, 16), column * 128 : column * 128 + 128]
+
+    value_send[HALF:] = jnp.zeros((2, 16, 128), bf16)
+    pair_copies = []
+    for row in range(18):
+        for column in range(9):
+            value_send[row * 9 + column] = value_tile(away, row, column).astype(bf16)
+    for k in range(4):
+        part = pl.ds(k * PART, PART)
+        pair_copies.append(send(other, value_send.at[part], value_got.at[part], pair_sem, k))
+    for row in range(18):
+        for column in range(9):
+            value_own[row * 9 + column] = value_tile(home, row, column)
+    value_own[HALF:] = jnp.zeros((2, 16, 128), f32)
+
+    rows_copy.wait_recv()
+    small_copy.wait_recv()
+    small_pair[...] = small_ref[...] + small_got[...]
+    rows_all[0, 0] = rows_ref[...]
+    rows_all[0, 1] = rows_got[...]
+    gathers = []
+    for step in (1, 2, 3):
+        device = first_peer(step)[0]
+        gathers.append(send(device, rows_all.at[0], rows_all.at[step], rows_sem, step))
+        gathers.append(send(device, small_pair, small_all.at[step - 1], small_sem, step))
+
+    for copy in pair_copies:
+        copy.wait_recv()
+    first_copies = []
+    for step in (2, 1, 3):
+        device, place = first_peer(step)
+        part = pl.ds(place * PART, PART)
+        first_send[step - 1] = (value_own[part] + value_got[part].astype(f32)).astype(bf16)
+        first_copies.append(
+            send(device, first_send.at[step - 1], first_got.at[step - 1], first_sem, step - 1)
+        )
+
+    for copy in gathers:
+        copy.wait_recv()
+    rows = rows_all[...].astype(f32).reshape(8, 16, D)
+    embedding_grads = rows[:, :8].reshape(64, D).astype(bf16)
+    pools[...] = rows[:, 8:, :ROWS].reshape(64, ROWS).T
+    for block in range(3):
+        at = pl.multiple_of(home + block * 96, 32)
+        term = jnp.dot(
+            pools[pl.ds(at, 96), :].astype(bf16), embedding_grads, preferred_element_type=f32
+        )
+        for row in range(6):
+            for column in range(9):
+                out_own[(block * 6 + row) * 9 + column] = term[
+                    row * 16 : row * 16 + 16, column * 128 : column * 128 + 128
+                ]
+    out_own[HALF:] = jnp.zeros((2, 16, 128), f32)
+    small = small_pair[...] + small_all[0] + small_all[1] + small_all[2]
+    grid[:, SLOTS:] = jnp.zeros((4, OWNED, 16, 128), f32)
+    for tile in range(5):
+        slot = (tile // OWNED, SLOTS + tile % OWNED)
+        grid[slot[0], slot[1], 0:8] = small[:, tile * 256 : tile * 256 + 128]
+        grid[slot[0], slot[1], 8:16] = small[:, tile * 256 + 128 : tile * 256 + 256]
+    mine = first * PART
+    grid[1, 20] = out_own[mine]
+    grid[2, 0:SLOTS] = out_own[pl.ds(mine + 1, 21)]
+    grid[3, 0:19] = out_own[pl.ds(mine + 22, 19)]
+    grid[3, 19:SLOTS] = jnp.zeros((2, 16, 128), f32)
+
+    for copy in first_copies:
+        copy.wait_recv()
+
+    def value_sum(start, count):
+        part = pl.ds(mine + start, count)
+        acc = value_own[part] + value_got[part].astype(f32)
+        for slot in range(3):
+            acc = acc + first_got[slot, start : start + count].astype(f32)
+        return acc
+
+    grid[0, 0:SLOTS] = value_sum(0, 21)
+    grid[1, 0:20] = value_sum(21, 20)
+
+    second_copies = []
+    for step in (2, 1, 3):
+        device, place = second_peer(step)
+        second_copies.append(
+            send(device, grid.at[place], second_got.at[step - 1], second_sem, step - 1)
+        )
+    for copy in second_copies:
+        copy.wait_recv()
+    total[...] = grid[second] + second_got[0] + second_got[1] + second_got[2]
+
+    third_copies = []
+    for step in (4, 3, 5, 2, 6, 1, 7):
+        device, place = third_peer(step)
+        third_copies.append(
+            send(device, total.at[pl.ds(place * OWNED, OWNED)], third_got.at[step - 1], third_sem, step - 1)
+        )
+    for copy in third_copies:
+        copy.wait_recv()
+    result = total[pl.ds(z * OWNED, OWNED)]
+    for slot in range(7):
+        result = result + third_got[slot]
+
+    owned[...] = result.astype(bf16)
+    small_owned[...] = result
+    owned_all[pl.ds(z * OWNED, OWNED)] = result.astype(bf16)
+    target = owned_all.at[pl.ds(z * OWNED, OWNED)]
+
+    @pl.when(z == 7)
+    def _():
+        small_slots[second] = result
+        for step in range(1, 8):
+            device = third_peer(step)[0]
+            copy_to(device, small_owned, small_slots.at[second], back_small_sem, step - 1).start()
+        for step in range(1, 8):
+            device = third_peer(step)[0]
+            copy_to(device, small_owned, small_slots.at[second], back_small_sem, step - 1).wait_send()
+
+    @pl.when(z < 7)
+    def _():
+        for step in (4, 3, 5, 2, 6, 1, 7):
+            device = third_peer(step)[0]
+            copy_to(device, owned, target, back_sem, step - 1).start()
+        for step in range(1, 8):
+            device = third_peer(step)[0]
+            copy_to(device, owned, target, back_sem, step - 1).wait_send()
+
+    for step in range(1, 8):
+        device = third_peer(step)[0]
+        source = (z + 8 - step) % 8
+
+        @pl.when(source == 7)
+        def _():
+            copy_to(device, small_owned, small_slots.at[second], back_small_sem, step - 1).wait_recv()
+
+        @pl.when(source < 7)
+        def _():
+            arrived = owned_all.at[pl.ds(source * OWNED, OWNED)]
+            copy_to(device, owned, arrived, back_sem, step - 1).wait_recv()
+
+    final[core, first, second] = owned_all[0:SLOTS]
+    spread = []
+    for step in (2, 1, 3):
+        device = second_peer(step)[0]
+        spread.append(
+            send(device, owned_all.at[0:SLOTS], final.at[core, first, second], spread_sem, step - 1)
+        )
+    for step in (2, 1, 3):
+        device = second_peer(step)[0]
+        spread.append(
+            send(device, small_slots.at[second], small_slots.at[second], spread_small_sem, step - 1)
+        )
+    for copy in spread:
+        copy.wait_recv()
+
+    homes = []
+    mine = final.at[core, first]
+    for step in (2, 1, 3):
+        device = first_peer(step)[0]
+        homes.append(send(device, mine, mine, home_sem, step - 1))
+    cross = [send(other, mine, mine, cross_sem, 0)]
+
+    for tile in range(5):
+        slot = small_slots[tile // OWNED, tile % OWNED]
+        small_out[:, tile * 256 : tile * 256 + 128] = slot[0:8]
+        small_out[:, tile * 256 + 128 : tile * 256 + 256] = slot[8:16]
+
+    for copy, step in zip(homes[1:] + homes[:1], (1, 3, 2)):
+        copy.wait_recv()
+        part = final.at[core, (first + 4 - step) % 4]
+        cross.append(send(other, part, part, cross_sem, step))
+
+    def unpack(which):
+        for tile in range(HALF):
+            place, at = tile // PART, tile % PART
+            row = pl.ds(pl.multiple_of(which * 288 + tile // 9 * 16, 16), 16)
+            column = tile % 9 * 128
+            value_out[row, column : column + 128] = final[which, place, at // SLOTS, at % SLOTS]
+            at = at + PART
+            out_out[row, column : column + 128] = final[which, place, at // SLOTS, at % SLOTS]
+
+    unpack(core)
+    for copy in cross:
+        copy.wait_recv()
+    unpack(1 - core)
+    for copy in sent:
+        copy.wait_send()
+
+
+def reduce_all(value_part, rows, small_part):
+    f32, bf16 = jnp.float32, jnp.bfloat16
+    vmem = pl.BlockSpec(memory_space=pltpu.VMEM)
+    dma = pltpu.SemaphoreType.DMA
+    return pl.pallas_call(
+        reduce_kernel,
+        out_shape=(
+            jax.ShapeDtypeStruct((ROWS, D), bf16),
+            jax.ShapeDtypeStruct((ROWS, D), bf16),
+            jax.ShapeDtypeStruct((8, WIDE), f32),
+        ),
+        in_specs=[vmem] * 3,
+        out_specs=[vmem] * 3,
+        scratch_shapes=[
+            pltpu.VMEM((4 * PART, 16, 128), bf16),
+            pltpu.VMEM((4 * PART, 16, 128), bf16),
+            pltpu.VMEM((4 * PART, 16, 128), f32),
+            pltpu.VMEM((4, 2, 16, D), bf16),
+            pltpu.VMEM((16, D), bf16),
+            pltpu.VMEM((8, WIDE), f32),
+            pltpu.VMEM((8, WIDE), f32),
+            pltpu.VMEM((3, 8, WIDE), f32),
+            pltpu.VMEM((ROWS, 64), f32),
+            pltpu.VMEM((4 * PART, 16, 128), f32),
+            pltpu.VMEM((3, PART, 16, 128), bf16),
+            pltpu.VMEM((3, PART, 16, 128), bf16),
+            pltpu.VMEM((4, GRID, 16, 128), f32),
+            pltpu.VMEM((3, GRID, 16, 128), f32),
+            pltpu.VMEM((GRID, 16, 128), f32),
+            pltpu.VMEM((7, OWNED, 16, 128), f32),
+            pltpu.VMEM((OWNED, 16, 128), bf16),
+            pltpu.VMEM((GRID, 16, 128), bf16),
+            pltpu.VMEM((OWNED, 16, 128), f32),
+            pltpu.VMEM((4, OWNED, 16, 128), f32),
+            pltpu.VMEM((2, 4, 4, SLOTS, 16, 128), bf16),
+            dma((2, 4)),
+            dma((2, 4)),
+            dma((2, 4)),
+            dma((2, 3)),
+            dma((2, 3)),
+            dma((2, 7)),
+            dma((2, 7)),
+            dma((2, 7)),
+            dma((2, 3)),
+            dma((2, 3)),
+            dma((2, 3)),
+            dma((2, 4)),
+        ],
+        compiler_params=pltpu.CompilerParams(
+            collective_id=0, has_side_effects=True, vmem_limit_bytes=48 * 1024 * 1024
+        ),
+        name="reduce_all",
+    )(value_part, rows, small_part)
 
 
 norm_epsilon = 1e-06
@@ -82,7 +436,6 @@
         (image_total - image_unit * jnp.sum(image_unit * image_total, axis=-1, keepdims=True))
         / image_length
     ).astype(jnp.bfloat16)
-    out_part = jnp.einsum("nk,nd->kd", pooled, embedding_grad, preferred_element_type=jnp.float32)
     pooled_grad = jnp.einsum(
         "nd,kd->nk", embedding_grad, out_weight, preferred_element_type=jnp.float32
     ).reshape(count, HEADS, HEAD_DIM)
@@ -97,25 +450,26 @@
         .astype(jnp.bfloat16)
         .reshape(count * PATCHES, HEADS * HEAD_DIM)
     )
-    value_part = jnp.einsum("nc,nk->ck", flat, value_rows_grad, preferred_element_type=jnp.float32)
+    value_part = jnp.einsum("nk,nc->kc", value_rows_grad, flat, preferred_element_type=jnp.float32)
     score_low = score_grad.astype(jnp.bfloat16)
-    patch_part = jnp.einsum("ipc,ihp->ch", patches, score_low, preferred_element_type=jnp.float32)
+    patch_part = jnp.einsum("ihp,ipc->hc", score_low, patches, preferred_element_type=jnp.float32)
     probe_part = jnp.einsum(
         "ihp,iphd->hd", score_grad, key_heads, preferred_element_type=jnp.float32
     ) / math.sqrt(HEAD_DIM)
+    small_part = jnp.concatenate(
+        [patch_part, jnp.pad(probe_part, ((0, 0), (0, WIDE - D - HEAD_DIM)))], axis=1
+    )
+    rows = jnp.concatenate([embedding_grad, jnp.pad(pooled, ((0, 0), (0, D - ROWS)))], axis=0)
+    value_total, out_total, small_total = reduce_all(value_part, rows, small_part)
     probe = probe_query.astype(jnp.float32).reshape(HEADS, HEAD_DIM)
-    key_part = (patch_part[:, :, None] * probe[None, :, :] / math.sqrt(HEAD_DIM)).reshape(
-        D, HEADS * HEAD_DIM
-    )
-    key_total, value_total, out_total, probe_total = lax.psum(
-        (key_part, value_part, out_part, probe_part), "dp"
-    )
+    patch_sum = small_total[:, :D].T
+    key_total = (patch_sum[:, :, None] * probe[None, :, :] / math.sqrt(HEAD_DIM)).reshape(D, ROWS)
     return (
         caption_grad,
-        probe_total.reshape(HEADS * HEAD_DIM),
+        small_total[:, D : D + HEAD_DIM].reshape(ROWS),
         key_total.astype(jnp.bfloat16),
-        value_total.astype(jnp.bfloat16),
-        out_total.astype(jnp.bfloat16),
+        value_total.T,
+        out_total,
     )
 
 

time: 205 us -> 126 us (0.61)
  blocking collectives: 140 us -> 0 us
  Pallas kernels: 0 us -> 64.8 us
  starting transfers between devices: 19.4 us -> 11 us
  local copies, waits for them, and re-layouts: 5.85 us -> 9.32 us
  matrix products: 29.4 us -> 31.6 us
    psum x1 -> x0, blocking collectives: 140 us -> none  [on_device(): lax.psum((key_part, value_part, out_part, probe_part), 'dp')]
    pallas_call x0 -> x1, Pallas kernels: none -> 64.8 us  [reduce_all(): pl.pallas_call(reduce_kernel, out_shape=(jax.ShapeDtypeStruct((ROWS, D),...]
    ppermute x5, starting transfers between devices: 19.4 us -> 11 us  [passed_along(): return lax.ppermute(block, axis, route)]
    dot_general x3 -> x2, matrix products: 12.3 us -> 8.63 us  [the longest x1 5.54 us: on_device(): jnp.einsum('nk,nc->kc', value_rows_grad, flat, preferred_element_type=jnp...]
    unnamed x21, local copies, waits for them, and re-layouts: 4.66 us -> 8.22 us
    dot_general x1, matrix products: 3.46 us -> 5.86 us  [on_device(): jnp.dot(flat, value_weight, preferred_element_type=jnp.float32)]
  transfers between devices with their start and end apart: 5 -> 5, of which waited for: 1 -> 1; matrix products, arithmetic and copies ran while one was open for 19% -> 33% of each run, Pallas kernels for 0% -> 52%
where the time goes in v1:
time: 126 us; the launch traced here: 125 us
  Pallas kernels  64.8 us (51%)
  matrix products  31.6 us (25%)
  starting transfers between devices  11 us (9%)
  local copies, waits for them, and re-layouts  9.32 us (7%)
  other arithmetic  5.88 us (5%)
  between operations  2.21 us (2%)
    pallas_call x1, Pallas kernels, reduce_all(): pl.pallas_call(reduce_kernel, out_shape=(jax.ShapeDtypeStruct((ROWS, D),...  64.8 us
    ppermute x5, starting transfers between devices, passed_along(): return lax.ppermute(block, axis, route)  11 us
    unnamed x21, local copies, waits for them, and re-layouts  8.22 us
    dot_general x1, matrix products, on_device(): jnp.dot(flat, value_weight, preferred_element_type=jnp.float32)  5.86 us
    dot_general x1, matrix products, on_device(): jnp.dot(flat, key_weight, preferred_element_type=jnp.float32)  5.84 us
    dot_general x1, matrix products, on_device(): jnp.einsum('nk,nc->kc', value_rows_grad, flat, preferred_element_type=jnp...  5.54 us
    dot_general x1, matrix products, on_device(): jnp.einsum('ihp,ipc->hc', score_low, patches, preferred_element_type=jnp....  3.09 us
    dot_general x1, matrix products, on_device(): jnp.einsum('ihd,iphd->ihp', pooled_grad, value_heads, preferred_element_t...  2.58 us
  transfers between devices with their start and end apart: 5, of which 1 were waited for; matrix products, arithmetic and copies ran while one was open for 33% of the time, Pallas kernels for 52%

profile of v1, /device:TPU:1, one launch (start us, length us, event | category | flops | bytes accessed | tf_op | source)
XLA Modules:
  0.0 125.1 jit_solution(9487676696485032506)
XLA Ops:
  0.6 2.7 %collective-permute-start.1 = (bf16[8,1152]{1,0:T(8,128)(2,1)}, bf16[8,1152]{1,0:T(8,128)(2,1)S(1)}, u32[]{:S(2)}, u32[]{:S(2)}) collective-permute-start(bf16[8,1152]{1,0:T(8,128)(2,1)} %param.9), channel_id=1, source_target_pairs={{255,0},{0,1},{1,2},{2,3},{3,4},{4,5},{5,6},{6,7},{7,8},{8,9},{9,1... | collective-permute-start | bytes 55304 | tf_op jit(solution)/shard_map/ppermute | solution.py:375
  3.3 0.9 fusion.37
  4.2 5.8 %convolution_convert_fusion.1 = bf16[2048,576]{0,1:T(8,128)(2,1)S(1)} fusion(bf16[2048,1152]{1,0:T(8,128)(2,1)} %bitcast.101, bf16[1152,576]{0,1:T(8,128)(2,1)S(1)} %copy-done), kind=kOutput, calls=%fused_computation.3 | convolution fusion | flops 2719088640 | bytes 8404992 | tf_op jit(solution)/shard_map/dot_general | solution.py:391
  10.1 2.2 %copy.26 = bf16[72,8,8,256]{3,2,1,0:T(8,128)(2,1)} copy(bf16[72,8,8,256]{3,1,2,0:T(8,128)(2,1)S(1)} %bitcast.107) | data formatting | bytes 4718592
  12.4 2.2 %fusion.11 = f32[8,1,8,256]{3,1,2,0:T(1,128)S(1)} fusion(bf16[8,72,1,1]{1,2,3,0:T(2,128)(2,1)S(1)} %reshape.87, bf16[8,256,8,72]{1,0,3,2:T(8,128)(2,1)} %bitcast.104), kind=kOutput, calls=%fused_computation.21 | convolution fusion | flops 2359296 | bytes 2425984 | tf_op jit(solution)/shard_map/iphd,hd->ihp/dot_general | solution.py:400
  14.6 1.3 %fusion.51 = (f32[8,8]{1,0:T(8,128)S(1)}, f32[8,8,256]{2,1,0:T(8,128)S(1)}) fusion(f32[8,1,8,256]{3,1,2,0:T(1,128)S(1)} %fusion.11), kind=kOutput, calls=%fused_computation.91 | output fusion | flops 49407 | bytes 131328 | tf_op jit(solution)/shard_map/sub | solution.py:403
  15.9 5.9 %convolution_convert_fusion = bf16[2048,576]{0,1:T(8,128)(2,1)S(1)} fusion(bf16[2048,1152]{1,0:T(8,128)(2,1)} %bitcast.102, bf16[1152,576]{0,1:T(8,128)(2,1)S(1)} %copy-done.7), kind=kOutput, calls=%fused_computation.2 | convolution fusion | flops 2719088640 | bytes 8404992 | tf_op jit(solution)/shard_map/dot_general | solution.py:396
  21.8 0.8 copy.27
  22.7 1.3 %copy-done.3 = bf16[72,8,8,256]{3,2,1,0:T(8,128)(2,1)} copy-done((bf16[72,8,8,256]{3,2,1,0:T(8,128)(2,1)}, bf16[72,8,8,256]{3,2,1,0:T(8,128)(2,1)S(1)}, u32[]{:S(2)}) %copy-start.3) | copy-done | bytes 2359320
  23.9 0.8 fusion.7
  27.9 1.5 %collective-permute-start.3 = (bf16[8,1152]{1,0:T(8,128)(2,1)S(1)}, bf16[8,1152]{1,0:T(8,128)(2,1)S(1)}, u32[]{:S(2)}, u32[]{:S(2)}) collective-permute-start(bf16[8,1152]{1,0:T(8,128)(2,1)S(1)} %collective-permute-done.1), channel_id=1, source_target_pairs={{255,0},{0,1},{1,2},{2,3},{3,4},{4,5},{5,6},{6,7},{7,8},{8,9},{9,1... | collective-permute-start | bytes 55304 | tf_op jit(solution)/shard_map/ppermute | solution.py:375
  31.7 2.6 %fusion.5 = f32[8,8,1,256]{3,2,1,0:T(1,128)S(1)} fusion(f32[8,8,72,1]{2,3,1,0:T(1,128)S(1)} %bitcast.110, bf16[8,256,8,72]{1,0,3,2:T(8,128)(2,1)} %bitcast.99), kind=kOutput, calls=%fused_computation.15 | convolution fusion | flops 2359296 | bytes 2443264 | tf_op jit(solution)/shard_map/ihd,iphd->ihp/dot_general | solution.py:442
  34.4 3.1 %convolution_bitcast_fusion = f32[8,1152]{1,0:T(8,128)S(1)} fusion(bf16[8,256,1152]{2,1,0:T(8,128)(2,1)} %param.8, f32[8,8,256]{2,1,0:T(8,128)S(1)} %get-tuple-element.12, f32[8,8,1,256]{3,2,1,0:T(1,128)S(1)} %fusion.5, f32[8,8]{1,0:T(8,128)S(1)} %fusion.32), kind=kOutput, calls=%fused_computation.14 | convolution fusion | flops 37797888 | bytes 4886784 | tf_op jit(solution)/shard_map/ihp,ipc->hc/dot_general | solution.py:455
  37.8 2.4 %fusion.9 = f32[8,1,72,1]{2,1,3,0:T(1,128)S(1)} fusion(bf16[8,256,8,72]{1,0,3,2:T(8,128)(2,1)} %bitcast.105, bf16[8,8,256,1]{2,1,0,3:T(8,128)(2,1)S(1)} %fusion.43), kind=kOutput, calls=%fused_computation.19 | convolution fusion | flops 2359296 | bytes 2394368 | tf_op jit(solution)/shard_map/ihp,iphd->hd/dot_general | solution.py:456
  40.2 0.8 multiply_convert_fusion
  40.9 0.8 copy.28
  41.7 5.5 %fusion.53.value_ref = f32[576,1152]{1,0:T(8,128)S(1)} fusion(bf16[2048,576]{0,1:T(8,128)(2,1)S(1)} %bitcast.106, bf16[2048,1152]{1,0:T(8,128)(2,1)} %bitcast.103), kind=kOutput, calls=%fused_computation.93 | convolution fusion | flops 2717908992 | bytes 9732096 | tf_op jit(solution)/shard_map/nk,nc->kc/dot_general | solution.py:453
  47.8 2.4 %collective-permute-start.2 = (f32[8,1152]{1,0:T(8,128)S(1)}, f32[8,1152]{1,0:T(8,128)S(1)}, u32[]{:S(2)}, u32[]{:S(2)}) collective-permute-start(f32[8,1152]{1,0:T(8,128)S(1)} %fusion.4), channel_id=1, source_target_pairs={{255,0},{0,1},{1,2},{2,3},{3,4},{4,5},{5,6},{6,7},{7,8},{8,9},{9,1... | collective-permute-start | bytes 110600 | tf_op jit(solution)/shard_map/ppermute | solution.py:375
  50.2 64.8 %reduce_all.1 = (bf16[576,1152]{1,0:T(8,128)(2,1)S(1)}, bf16[576,1152]{1,0:T(8,128)(2,1)S(1)}, f32[8,1280]{1,0:T(8,128)S(1)}) custom-call(f32[576,1152]{1,0:T(8,128)S(1)} %fusion.53.value_ref, bf16[16,1152]{1,0:T(8,128)(2,1)S(1)} %fusion.40.rows_ref, f32[8,1280]{1,0:T(8,128)S(1)} %select_maximum_fusion.small_ref), custom_call_target="tpu_custom_call" | custom-call | tf_op jit(solution)/shard_map/reduce_all/pallas_call | solution.py:318
  115.0 1.1 copy-done.1
  116.0 4.0 %collective-permute-start.4 = (f32[8,1152]{1,0:T(8,128)S(1)}, f32[8,1152]{1,0:T(8,128)S(1)}, u32[]{:S(2)}, u32[]{:S(2)}) collective-permute-start(f32[8,1152]{1,0:T(8,128)S(1)} %add.83), channel_id=1, source_target_pairs={{2,0},{3,1},{4,2},{5,3},{6,4},{7,5},{8,6},{9,7},{10,8},{11,9},{12,... | collective-permute-start | bytes 110600 | tf_op jit(solution)/shard_map/ppermute | solution.py:375
  120.8 1.4 %fusion.2 = bf16[1152,576]{0,1:T(8,128)(2,1)} fusion(f32[576]{0:T(1024)S(1)} %convert_element_type.58, f32[1152,8]{0,1:T(8,128)S(1)} %slice_bitcast_fusion), kind=kLoop, calls=%fused_computation.6 | loop fusion | flops 1990656 | bytes 1366272 | tf_op jit(solution)/shard_map/convert_element_type | solution.py:470
  123.0 1.1 copy.60
  124.1 1.1 copy.61
  (56 shorter events, 6.8 us)
Async XLA Ops:
  0.6 3.6 %copy-start = (bf16[1152,576]{0,1:T(8,128)(2,1)S(1)}, bf16[1152,576]{0,1:T(8,128)(2,1)}, u32[]{:S(2)}) copy-start(bf16[1152,576]{0,1:T(8,128)(2,1)} %param.11) | copy-start | bytes 3981316
  0.6 27.2 %collective-permute-start.1 = (bf16[8,1152]{1,0:T(8,128)(2,1)}, bf16[8,1152]{1,0:T(8,128)(2,1)S(1)}, u32[]{:S(2)}, u32[]{:S(2)}) collective-permute-start(bf16[8,1152]{1,0:T(8,128)(2,1)} %param.9), channel_id=1, source_target_pairs={{255,0},{0,1},{1,2},{2,3},{3,4},{4,5},{5,6},{6,7},{7,8},{8,9},{9,1... | collective-permute-start | bytes 55304 | tf_op jit(solution)/shard_map/ppermute | solution.py:375
  10.1 2.2 %copy-start.6 = (bf16[576]{0:T(1024)(128)(2,1)S(1)}, bf16[576]{0:T(1024)(128)(2,1)}, u32[]{:S(2)}) copy-start(bf16[576]{0:T(1024)(128)(2,1)} %param.10) | copy-start | bytes 3460
  12.3 3.6 %copy-start.7 = (bf16[1152,576]{0,1:T(8,128)(2,1)S(1)}, bf16[1152,576]{0,1:T(8,128)(2,1)}, u32[]{:S(2)}) copy-start(bf16[1152,576]{0,1:T(8,128)(2,1)} %param.12) | copy-start | bytes 3981316
  22.5 1.4 %copy-start.3 = (bf16[72,8,8,256]{3,2,1,0:T(8,128)(2,1)}, bf16[72,8,8,256]{3,2,1,0:T(8,128)(2,1)S(1)}, u32[]{:S(2)}) copy-start(bf16[72,8,8,256]{3,2,1,0:T(8,128)(2,1)S(1)} %copy.27) | copy-start | bytes 7077892
  22.5 3.6 %copy-start.4 = (bf16[576,1152]{1,0:T(8,128)(2,1)S(1)}, bf16[576,1152]{1,0:T(8,128)(2,1)}, u32[]{:S(2)}) copy-start(bf16[576,1152]{1,0:T(8,128)(2,1)} %param.13) | copy-start | bytes 3981316
  22.6 4.0 %copy-start.5 = (bf16[8,1152]{1,0:T(8,128)(2,1)S(1)}, bf16[8,1152]{1,0:T(8,128)(2,1)}, u32[]{:S(2)}) copy-start(bf16[8,1152]{1,0:T(8,128)(2,1)} %param.9) | copy-start | bytes 55300
  27.1 20.5 %collective-permute-start = (f32[8,1152]{1,0:T(8,128)S(1)}, f32[8,1152]{1,0:T(8,128)S(1)}, u32[]{:S(2)}, u32[]{:S(2)}) collective-permute-start(f32[8,1152]{1,0:T(8,128)S(1)} %convolution_multiply_fusion.2), channel_id=1, source_target_pairs={{255,0},{0,1},{1,2},{2,3},{3,4},{4,5},{5,6},{6,7},{7,8},{8,9},{9,1... | collective-permute-start | bytes 110600 | tf_op jit(solution)/shard_map/ppermute | solution.py:375
  27.9 2.4 %collective-permute-start.3 = (bf16[8,1152]{1,0:T(8,128)(2,1)S(1)}, bf16[8,1152]{1,0:T(8,128)(2,1)S(1)}, u32[]{:S(2)}, u32[]{:S(2)}) collective-permute-start(bf16[8,1152]{1,0:T(8,128)(2,1)S(1)} %collective-permute-done.1), channel_id=1, source_target_pairs={{255,0},{0,1},{1,2},{2,3},{3,4},{4,5},{5,6},{6,7},{7,8},{8,9},{9,1... | collective-permute-start | bytes 55304 | tf_op jit(solution)/shard_map/ppermute | solution.py:375
  47.8 68.2 %collective-permute-start.2 = (f32[8,1152]{1,0:T(8,128)S(1)}, f32[8,1152]{1,0:T(8,128)S(1)}, u32[]{:S(2)}, u32[]{:S(2)}) collective-permute-start(f32[8,1152]{1,0:T(8,128)S(1)} %fusion.4), channel_id=1, source_target_pairs={{255,0},{0,1},{1,2},{2,3},{3,4},{4,5},{5,6},{6,7},{7,8},{8,9},{9,1... | collective-permute-start | bytes 110600 | tf_op jit(solution)/shard_map/ppermute | solution.py:375
  115.0 1.1 copy-start.1
  116.0 6.1 %collective-permute-start.4 = (f32[8,1152]{1,0:T(8,128)S(1)}, f32[8,1152]{1,0:T(8,128)S(1)}, u32[]{:S(2)}, u32[]{:S(2)}) collective-permute-start(f32[8,1152]{1,0:T(8,128)S(1)} %add.83), channel_id=1, source_target_pairs={{2,0},{3,1},{4,2},{5,3},{6,4},{7,5},{8,6},{9,7},{10,8},{11,9},{12,... | collective-permute-start | bytes 110600 | tf_op jit(solution)/shard_map/ppermute | solution.py:375
  120.8 2.3 %copy-start.2 = (bf16[576,1152]{1,0:T(8,128)(2,1)S(1)}, bf16[576,1152]{1,0:T(8,128)(2,1)}, u32[]{:S(2)}) copy-start(bf16[576,1152]{1,0:T(8,128)(2,1)} %copy-done.1) | copy-start | bytes 3981316

commit v2 on v1

v2 whole, which is shorter than its diff:
```python
import math

import jax
import jax.numpy as jnp
from jax import lax
from jax.experimental import pallas as pl
from jax.experimental.pallas import tpu as pltpu
from jax.sharding import PartitionSpec as P

D = 1152
HEADS = 8
HEAD_DIM = 72
PATCHES = 256
IMG_DEV = 8
ROWS = HEADS * HEAD_DIM
FLAT = IMG_DEV * PATCHES
CHUNK = 512

MESH = pl.DeviceIdType.MESH
HALF = 162
HALF_ROWS = 288
PART = 41
SLOTS = 21
OWNED = 3
GRID = 24
WIDE = 1792
SMALL_TILES = WIDE // 256

norm_epsilon = 1e-06


def normalize(rows):
    length = jnp.sqrt(jnp.sum(rows * rows, axis=-1, keepdims=True) + norm_epsilon)
    return (rows / length, length)


def dot(left, right, left_dim=1, right_dim=0, precision=None):
    dims = (((left_dim,), (right_dim,)), ((), ()))
    return lax.dot_general(left, right, dims, precision=precision, preferred_element_type=jnp.float32)


def split_low(values):
    high = values.astype(jnp.bfloat16).astype(jnp.float32)
    return jnp.concatenate([high, values - high], axis=0).astype(jnp.bfloat16)


def whole_kernel(
    scale_ref,
    bias_ref,
    patches_ref,
    captions_ref,
    probe_ref,
    key_ref,
    value_ref,
    out_ref,
    caption_out,
    key_out,
    probe_out,
    value_out,
    out_out,
    x_all,
    key_weight,
    value_weight,
    out_weight,
    keys,
    values,
    scores,
    attention,
    units,
    backs,
    backs_got,
    turned,
    rows_wide,
    rows_own,
    away_rows,
    home_rows,
    score_rows,
    small_own,
    value_send,
    value_got,
    value_own,
    rows_all,
    rows_got,
    small_got,
    small_pair,
    small_all,
    pools,
    out_own,
    first_send,
    first_got,
    grid,
    second_got,
    total,
    third_got,
    owned,
    owned_all,
    small_owned,
    small_slots,
    final,
    load_sem,
    unit_sem,
    visit_sem,
    pair_sem,
    rows_sem,
    small_sem,
    first_sem,
    second_sem,
    third_sem,
    back_sem,
    back_small_sem,
    spread_sem,
    spread_small_sem,
    home_sem,
    cross_sem,
):
    f32, bf16 = jnp.float32, jnp.bfloat16
    highest = lax.Precision.HIGHEST
    me = lax.axis_index("dp")
    core, x, y, z = me % 2, (me // 2) % 4, (me // 8) % 4, me // 32
    first = x + (y - x) * core
    second = y + (x - y) * core

    def device_at(at_z, at_first, at_second, at_core):
        at_x = at_first + (at_second - at_first) * core
        at_y = at_second + (at_first - at_second) * core
        return ((at_z * 4 + at_y) * 4 + at_x) * 2 + at_core

    other = device_at(z, first, second, 1 - core)

    def first_peer(step):
        place = (first + step) % 4
        return device_at(z, place, second, core), place

    def second_peer(step):
        place = (second + step) % 4
        return device_at(z, first, place, core), place

    def third_peer(step):
        place = (z + step) % 8
        return device_at(place, first, second, core), place

    peers = [other]
    peers += [first_peer(step)[0] for step in (1, 2, 3)]
    peers += [second_peer(step)[0] for step in (1, 2, 3)]
    peers += [third_peer(step)[0] for step in range(1, 8)]
    peers += [(me + step) % 256 for step in (1, 2, 254, 255)]
    barrier = pltpu.get_barrier_semaphore()
    for peer in peers:
        pl.semaphore_signal(barrier, inc=1, device_id=(peer,), device_id_type=MESH)

    def load(source, target, slot):
        return pltpu.make_async_copy(source, target, load_sem.at[slot])

    def load_rows(slot):
        part = pl.ds(pl.multiple_of(slot * CHUNK, CHUNK), CHUNK)
        return load(patches_ref.at[part], x_all.at[part], slot)

    load(key_ref, key_weight, 4).start()
    load_rows(0).start()
    load(value_ref, value_weight, 5).start()
    for slot in (1, 2, 3):
        load_rows(slot).start()
    load(out_ref, out_weight, 6).start()

    sent = []

    def copy_to(device, source, target, sems, slot):
        return pltpu.make_async_remote_copy(
            src_ref=source,
            dst_ref=target,
            send_sem=sems.at[0, slot],
            recv_sem=sems.at[1, slot],
            device_id=(device,),
            device_id_type=MESH,
        )

    def send(*where):
        copy = copy_to(*where)
        copy.start()
        sent.append(copy)
        return copy

    head = lax.broadcasted_iota(jnp.int32, (HEADS, ROWS), 0) * HEAD_DIM
    column = lax.broadcasted_iota(jnp.int32, (HEADS, ROWS), 1)
    own_head = (column >= head) & (column < head + HEAD_DIM)
    probe = jnp.where(own_head, jnp.broadcast_to(probe_ref[...].astype(f32), (HEADS, ROWS)), 0.0)
    probe_low = probe.astype(bf16)

    def project(step, unused):
        load_rows(step).wait()
        part = pl.ds(pl.multiple_of(step * CHUNK, CHUNK), CHUNK)
        rows = x_all[part, :]
        key_rows = dot(rows, key_weight[...]).astype(bf16)
        keys[part, :] = key_rows
        values[part, :] = dot(rows, value_weight[...]).astype(bf16)
        score = dot(probe_low, key_rows, 1, 1)
        at = pl.multiple_of(step * 16, 16)
        scores[pl.ds(at, 8), :] = score[:, :PATCHES]
        scores[pl.ds(at + 8, 8), :] = score[:, PATCHES:]
        return unused

    load(key_ref, key_weight, 4).wait()
    load(value_ref, value_weight, 5).wait()
    lax.fori_loop(0, 3, project, 0)
    own_unit, own_length = normalize(captions_ref[...].astype(f32))
    units[0] = own_unit
    pl.semaphore_wait(barrier, len(peers))
    unit_copies = [
        send((me + step) % 256, units.at[0], units.at[step], unit_sem, step - 1) for step in (1, 2)
    ]
    lax.fori_loop(3, 4, project, 0)

    score = scores[...] / math.sqrt(HEAD_DIM)
    raised = jnp.exp(score - jnp.max(score, axis=-1, keepdims=True))
    attend = raised / jnp.sum(raised, axis=-1, keepdims=True)
    attention[...] = attend
    pooled = []
    for image in range(IMG_DEV):
        weights = attend[image * 8 : image * 8 + 8].astype(bf16)
        mixed = dot(weights, values[image * PATCHES : (image + 1) * PATCHES, :])
        pooled.append(jnp.sum(jnp.where(own_head, mixed, 0.0), axis=0, keepdims=True))
    pooled = jnp.concatenate(pooled, axis=0)
    load(out_ref, out_weight, 6).wait()
    embedding = dot(pooled.astype(bf16), out_weight[...])
    image_unit, image_length = normalize(embedding)

    for copy in unit_copies:
        copy.wait_recv()
    caption_units = units[...].reshape(24, D)
    scale, bias = scale_ref[0], bias_ref[0]
    logits = scale * dot(image_unit, caption_units, 1, 1, highest) + bias
    same = lax.broadcasted_iota(jnp.int32, (8, 24), 0) == lax.broadcasted_iota(jnp.int32, (8, 24), 1)
    slope = jax.nn.sigmoid(logits) - jnp.where(same, 1.0, 0.0)
    image_total = scale * dot(slope, caption_units, 1, 0, highest)
    embedding_grad = (
        image_total - image_unit * jnp.sum(image_unit * image_total, axis=-1, keepdims=True)
    ) / image_length
    rows_wide[...] = jnp.zeros((16, D), f32)
    rows_wide[0:8, :] = embedding_grad
    rows_wide[8:16, 0:ROWS] = pooled
    rows_own[...] = rows_wide[...].astype(bf16)
    rows_copy = send(other, rows_own, rows_got, rows_sem, 0)
    backs[...] = (scale * dot(slope, image_unit, 0, 0, highest)).reshape(3, 8, D)
    visit_copies = [
        send((me + 256 - step) % 256, backs.at[step], backs_got.at[step - 1], visit_sem, step - 1)
        for step in (1, 2)
    ]

    grad_low = embedding_grad.astype(bf16)
    pooled_grad = dot(grad_low, out_weight[...], 1, 1)
    turned[...] = dot(out_weight[...], grad_low, 1, 1)
    attention_grad = []
    for image in range(IMG_DEV):
        spread_grad = jnp.where(
            own_head, jnp.broadcast_to(pooled_grad[image : image + 1], (HEADS, ROWS)), 0.0
        )
        both = dot(split_low(spread_grad), values[image * PATCHES : (image + 1) * PATCHES, :], 1, 1)
        attention_grad.append(both[0:8] + both[8:16])
    attention_grad = jnp.concatenate(attention_grad, axis=0)
    score_grad = attend * (
        attention_grad - jnp.sum(attend * attention_grad, axis=-1, keepdims=True)
    )

    def value_rows_grad(start, target):
        for image in range(IMG_DEV):
            for pair in range(2):
                parts = []
                for place in (2 * pair, 2 * pair + 1):
                    at = start + place
                    grads = turned[pl.ds(pl.multiple_of(at * HEAD_DIM, 8), HEAD_DIM), image : image + 1]
                    parts.append(grads * attention[pl.ds(image * 8 + at, 1), :])
                target[pair * 144 : pair * 144 + 144, image * PATCHES : (image + 1) * PATCHES] = (
                    jnp.concatenate(parts, axis=0).astype(bf16)
                )

    value_rows_grad((1 - core) * 4, away_rows)
    for image in range(IMG_DEV):
        part = score_grad[image * 8 : image * 8 + 8]
        lanes = slice(image * PATCHES, (image + 1) * PATCHES)
        away_rows[HALF_ROWS : HALF_ROWS + 16, lanes] = jnp.concatenate(
            [part, jnp.zeros((8, PATCHES), f32)], axis=0
        ).astype(bf16)
        score_rows[:, lanes] = split_low(part)

    rows_copy.wait_recv()
    rows_all[0, 0] = rows_own[...]
    rows_all[0, 1] = rows_got[...]
    gathers = [
        send(first_peer(step)[0], rows_all.at[0], rows_all.at[step], rows_sem, step)
        for step in (1, 2, 3)
    ]

    value_send[HALF:] = jnp.zeros((2, 16, 128), bf16)
    pair_copies = []
    for block in range(5):
        lanes = slice(block * 256, min(block * 256 + 256, D))
        term = dot(away_rows[...], x_all[:, lanes])
        for tile in range(block * 36, min(block * 36 + 36, HALF)):
            row, lane = tile % 18 * 16, tile // 18 * 128 - block * 256
            value_send[tile] = term[row : row + 16, lane : lane + 128].astype(bf16)
        small_own[:, lanes] = term[HALF_ROWS : HALF_ROWS + 8]
        if block > 0:
            part = pl.ds((block - 1) * PART, PART)
            pair_copies.append(
                send(other, value_send.at[part], value_got.at[part], pair_sem, block - 1)
            )
    probe_part = dot(score_rows[...], keys[...])
    probe_part = jnp.where(own_head, probe_part[0:8] + probe_part[8:16], 0.0) / math.sqrt(HEAD_DIM)
    small_own[:, D:WIDE] = jnp.zeros((8, WIDE - D), f32)
    small_own[:, D : D + ROWS] = probe_part
    small_copy = send(other, small_own, small_got, small_sem, 0)

    value_rows_grad(core * 4, home_rows)
    for block in range(5):
        lanes = slice(block * 256, min(block * 256 + 256, D))
        term = dot(home_rows[...], x_all[:, lanes])
        for tile in range(block * 36, min(block * 36 + 36, HALF)):
            row, lane = tile % 18 * 16, tile // 18 * 128 - block * 256
            value_own[tile] = term[row : row + 16, lane : lane + 128]
    value_own[HALF:] = jnp.zeros((2, 16, 128), f32)

    small_copy.wait_recv()
    small_pair[...] = small_own[...] + small_got[...]
    gathers += [
        send(first_peer(step)[0], small_pair, small_all.at[step - 1], small_sem, step)
        for step in (1, 2, 3)
    ]

    for copy in pair_copies:
        copy.wait_recv()
    first_copies = []
    for step in (2, 1, 3):
        device, place = first_peer(step)
        part = pl.ds(place * PART, PART)
        first_send[step - 1] = (value_own[part] + value_got[part].astype(f32)).astype(bf16)
        first_copies.append(
            send(device, first_send.at[step - 1], first_got.at[step - 1], first_sem, step - 1)
        )

    for copy in gathers:
        copy.wait_recv()
    rows = rows_all[...].astype(f32).reshape(8, 16, D)
    embedding_grads = rows[:, :8].reshape(64, D).astype(bf16)
    pools[...] = rows[:, 8:, :ROWS].reshape(64, ROWS).T
    for block in range(3):
        at = pl.multiple_of(core * HALF_ROWS + block * 96, 32)
        term = jnp.dot(
            pools[pl.ds(at, 96), :].astype(bf16), embedding_grads, preferred_element_type=f32
        )
        for row in range(6):
            for column in range(9):
                out_own[column * 18 + block * 6 + row] = term[
                    row * 16 : row * 16 + 16, column * 128 : column * 128 + 128
                ]
    out_own[HALF:] = jnp.zeros((2, 16, 128), f32)
    small = small_pair[...] + small_all[0] + small_all[1] + small_all[2]
    grid[:, SLOTS:] = jnp.zeros((4, OWNED, 16, 128), f32)
    for tile in range(SMALL_TILES):
        slot = (tile // OWNED, SLOTS + tile % OWNED)
        grid[slot[0], slot[1], 0:8] = small[:, tile * 256 : tile * 256 + 128]
        grid[slot[0], slot[1], 8:16] = small[:, tile * 256 + 128 : tile * 256 + 256]
    mine = first * PART
    grid[1, 20] = out_own[mine]
    grid[2, 0:SLOTS] = out_own[pl.ds(mine + 1, 21)]
    grid[3, 0:19] = out_own[pl.ds(mine + 22, 19)]
    grid[3, 19:SLOTS] = jnp.zeros((2, 16, 128), f32)

    for copy in first_copies:
        copy.wait_recv()

    def value_sum(start, count):
        part = pl.ds(mine + start, count)
        acc = value_own[part] + value_got[part].astype(f32)
        for slot in range(3):
            acc = acc + first_got[slot, start : start + count].astype(f32)
        return acc

    grid[0, 0:SLOTS] = value_sum(0, 21)
    grid[1, 0:20] = value_sum(21, 20)

    second_copies = []
    for step in (2, 1, 3):
        device, place = second_peer(step)
        second_copies.append(
            send(device, grid.at[place], second_got.at[step - 1], second_sem, step - 1)
        )
    for copy in second_copies:
        copy.wait_recv()
    total[...] = grid[second] + second_got[0] + second_got[1] + second_got[2]

    third_copies = []
    for step in (4, 3, 5, 2, 6, 1, 7):
        device, place = third_peer(step)
        third_copies.append(
            send(device, total.at[pl.ds(place * OWNED, OWNED)], third_got.at[step - 1], third_sem, step - 1)
        )
    for copy in third_copies:
        copy.wait_recv()
    result = total[pl.ds(z * OWNED, OWNED)]
    for slot in range(7):
        result = result + third_got[slot]

    owned[...] = result.astype(bf16)
    small_owned[...] = result
    owned_all[pl.ds(z * OWNED, OWNED)] = result.astype(bf16)
    target = owned_all.at[pl.ds(z * OWNED, OWNED)]

    @pl.when(z == 7)
    def _():
        small_slots[second] = result
        for step in range(1, 8):
            device = third_peer(step)[0]
            copy_to(device, small_owned, small_slots.at[second], back_small_sem, step - 1).start()
        for step in range(1, 8):
            device = third_peer(step)[0]
            copy_to(device, small_owned, small_slots.at[second], back_small_sem, step - 1).wait_send()

    @pl.when(z < 7)
    def _():
        for step in (4, 3, 5, 2, 6, 1, 7):
            device = third_peer(step)[0]
            copy_to(device, owned, target, back_sem, step - 1).start()
        for step in range(1, 8):
            device = third_peer(step)[0]
            copy_to(device, owned, target, back_sem, step - 1).wait_send()

    for step in range(1, 8):
        device = third_peer(step)[0]
        source = (z + 8 - step) % 8

        @pl.when(source == 7)
        def _():
            copy_to(device, small_owned, small_slots.at[second], back_small_sem, step - 1).wait_recv()

        @pl.when(source < 7)
        def _():
            arrived = owned_all.at[pl.ds(source * OWNED, OWNED)]
            copy_to(device, owned, arrived, back_sem, step - 1).wait_recv()

    final[core, first, second] = owned_all[0:SLOTS]
    spread = []
    for step in (2, 1, 3):
        device = second_peer(step)[0]
        spread.append(
            send(device, owned_all.at[0:SLOTS], final.at[core, first, second], spread_sem, step - 1)
        )
    for step in (2, 1, 3):
        device = second_peer(step)[0]
        spread.append(
            send(device, small_slots.at[second], small_slots.at[second], spread_small_sem, step - 1)
        )
    for copy in spread:
        copy.wait_recv()

    homes = []
    mine = final.at[core, first]
    for step in (2, 1, 3):
        device = first_peer(step)[0]
        homes.append(send(device, mine, mine, home_sem, step - 1))
    cross = [send(other, mine, mine, cross_sem, 0)]

    small = []
    for tile in range(SMALL_TILES):
        slot = small_slots[tile // OWNED, tile % OWNED]
        small += [slot[0:8], slot[8:16]]
    patch_sum = jnp.concatenate(small[:9], axis=1)
    high = patch_sum.astype(bf16).astype(f32)
    middle = (patch_sum - high).astype(bf16).astype(f32)
    thirds = jnp.concatenate([high, middle, patch_sum - high - middle], axis=0).astype(bf16)
    probes = jnp.concatenate([probe] * 3, axis=0).astype(bf16)
    for block in range(3):
        part = slice(block * 384, block * 384 + 384)
        term = dot(thirds[:, part], probes, 0, 0) / math.sqrt(HEAD_DIM)
        key_out[part, :] = term.astype(bf16)
    probe_out[...] = jnp.sum(jnp.concatenate(small[9:], axis=1)[:, :ROWS], axis=0, keepdims=True)
    for copy in visit_copies:
        copy.wait_recv()
    caption_total = backs[0] + backs_got[0] + backs_got[1]
    caption_out[...] = (
        caption_total - own_unit * jnp.sum(own_unit * caption_total, axis=-1, keepdims=True)
    ) / own_length

    for copy, step in zip(homes[1:] + homes[:1], (1, 3, 2)):
        copy.wait_recv()
        part = final.at[core, (first + 4 - step) % 4]
        cross.append(send(other, part, part, cross_sem, step))

    def unpack(which):
        for tile in range(HALF):
            place, at = tile // PART, tile % PART
            row = pl.ds(pl.multiple_of(which * HALF_ROWS + tile % 18 * 16, 16), 16)
            column = tile // 18 * 128
            value_out[row, column : column + 128] = final[which, place, at // SLOTS, at % SLOTS]
            at = at + PART
            out_out[row, column : column + 128] = final[which, place, at // SLOTS, at % SLOTS]

    unpack(core)
    for copy in cross:
        copy.wait_recv()
    unpack(1 - core)
    for copy in sent:
        copy.wait_send()


def on_device(
    patches, captions, probe_query, key_weight, value_weight, out_weight, logit_scale, logit_bias
):
    f32, bf16 = jnp.float32, jnp.bfloat16
    vmem = pl.BlockSpec(memory_space=pltpu.VMEM)
    smem = pl.BlockSpec(memory_space=pltpu.SMEM)
    hbm = pl.BlockSpec(memory_space=pl.ANY)
    dma = pltpu.SemaphoreType.DMA
    caption_grad, key_grad, probe_grad, value_turned, out_grad = pl.pallas_call(
        whole_kernel,
        out_shape=(
            jax.ShapeDtypeStruct((IMG_DEV, D), f32),
            jax.ShapeDtypeStruct((D, ROWS), bf16),
            jax.ShapeDtypeStruct((1, ROWS), f32),
            jax.ShapeDtypeStruct((ROWS, D), bf16),
            jax.ShapeDtypeStruct((ROWS, D), bf16),
        ),
        in_specs=[smem, smem, hbm, vmem, vmem, hbm, hbm, hbm],
        out_specs=[vmem] * 5,
        scratch_shapes=[
            pltpu.VMEM((FLAT, D), bf16),
            pltpu.VMEM((D, ROWS), bf16),
            pltpu.VMEM((D, ROWS), bf16),
            pltpu.VMEM((ROWS, D), bf16),
            pltpu.VMEM((FLAT, ROWS), bf16),
            pltpu.VMEM((FLAT, ROWS), bf16),
            pltpu.VMEM((64, PATCHES), f32),
            pltpu.VMEM((64, PATCHES), f32),
            pltpu.VMEM((3, 8, D), f32),
            pltpu.VMEM((3, 8, D), f32),
            pltpu.VMEM((2, 8, D), f32),
            pltpu.VMEM((ROWS, 8), f32),
            pltpu.VMEM((16, D), f32),
            pltpu.VMEM((16, D), bf16),
            pltpu.VMEM((HALF_ROWS + 16, FLAT), bf16),
            pltpu.VMEM((HALF_ROWS, FLAT), bf16),
            pltpu.VMEM((16, FLAT), bf16),
            pltpu.VMEM((8, WIDE), f32),
            pltpu.VMEM((4 * PART, 16, 128), bf16),
            pltpu.VMEM((4 * PART, 16, 128), bf16),
            pltpu.VMEM((4 * PART, 16, 128), f32),
            pltpu.VMEM((4, 2, 16, D), bf16),
            pltpu.VMEM((16, D), bf16),
            pltpu.VMEM((8, WIDE), f32),
            pltpu.VMEM((8, WIDE), f32),
            pltpu.VMEM((3, 8, WIDE), f32),
            pltpu.VMEM((ROWS, 64), f32),
            pltpu.VMEM((4 * PART, 16, 128), f32),
            pltpu.VMEM((3, PART, 16, 128), bf16),
            pltpu.VMEM((3, PART, 16, 128), bf16),
            pltpu.VMEM((4, GRID, 16, 128), f32),
            pltpu.VMEM((3, GRID, 16, 128), f32),
            pltpu.VMEM((GRID, 16, 128), f32),
            pltpu.VMEM((7, OWNED, 16, 128), f32),
            pltpu.VMEM((OWNED, 16, 128), bf16),
            pltpu.VMEM((GRID, 16, 128), bf16),
            pltpu.VMEM((OWNED, 16, 128), f32),
            pltpu.VMEM((4, OWNED, 16, 128), f32),
            pltpu.VMEM((2, 4, 4, SLOTS, 16, 128), bf16),
            dma((7,)),
            dma((2, 2)),
            dma((2, 2)),
            dma((2, 4)),
            dma((2, 4)),
            dma((2, 4)),
            dma((2, 3)),
            dma((2, 3)),
            dma((2, 7)),
            dma((2, 7)),
            dma((2, 7)),
            dma((2, 3)),
            dma((2, 3)),
            dma((2, 3)),
            dma((2, 4)),
        ],
        compiler_params=pltpu.CompilerParams(
            collective_id=0, has_side_effects=True, vmem_limit_bytes=48 * 1024 * 1024
        ),
        name="whole",
    )(
        logit_scale,
        logit_bias,
        patches.reshape(FLAT, D),
        captions,
        probe_query.reshape(1, ROWS),
        key_weight,
        value_weight,
        out_weight,
    )
    return (caption_grad, probe_grad.reshape(ROWS), key_grad, value_turned.T, out_grad)


def solution(mesh):
    placed = (P("dp", None, None), P("dp", None), P(), P(), P(), P(), P(), P())
    return jax.shard_map(
        on_device,
        mesh=mesh,
        in_specs=placed,
        out_specs=(P("dp", None), P(), P(), P(), P()),
        check_vma=False,
    )
```

time: 126 us -> 95.2 us (0.76)
  matrix products: 31.6 us -> 0 us
  Pallas kernels: 64.8 us -> 80 us
  starting transfers between devices: 11 us -> 0 us
  other arithmetic: 5.88 us -> 0.6 us
  local copies, waits for them, and re-layouts: 9.32 us -> 12.4 us
    dot_general x19 -> x0, matrix products: 31.6 us -> none  [the longest x1 5.86 us: on_device(): jnp.dot(flat, value_weight, preferred_element_type=jnp.float32)]
    pallas_call x1, Pallas kernels: 64.8 us -> 80 us  [on_device(): pl.pallas_call(whole_kernel, out_shape=(jax.ShapeDtypeStruct((IMG_DEV, D)...]
    ppermute x5 -> x0, starting transfers between devices: 11 us -> none  [passed_along(): return lax.ppermute(block, axis, route)]
    unnamed x21 -> x20, local copies, waits for them, and re-layouts: 8.22 us -> 11.7 us
    convert_element_type x6 -> x0, other arithmetic: 2.32 us -> none  [the longest x1 1.36 us: on_device(): key_total.astype(jnp.bfloat16)]
    reduce_sum x5 -> x0, other arithmetic: 1.4 us -> none  [the longest x3 1.12 us: normalize(): jnp.sum(rows * rows, axis=-1, keepdims=True) + norm_epsilon]
    sub x1 -> x0, other arithmetic: 1.32 us -> none  [on_device(): attention = jax.nn.softmax(scores, axis=-1)]
  transfers between devices with their start and end apart: 5 -> 0, of which waited for: 1 -> 0; matrix products, arithmetic and copies ran while one was open for 33% -> 0% of each run, Pallas kernels for 52% -> 0%
where the time goes in v2:
time: 95.2 us; the launch traced here: 95 us
  Pallas kernels  80 us (84%)
  local copies, waits for them, and re-layouts  12.4 us (13%)
  between operations  1.95 us (2%)
    pallas_call x1, Pallas kernels, on_device(): pl.pallas_call(whole_kernel, out_shape=(jax.ShapeDtypeStruct((IMG_DEV, D)...  80 us
    unnamed x20, local copies, waits for them, and re-layouts  11.7 us

profile of v2, /device:TPU:1, one launch (start us, length us, event | category | flops | bytes accessed | tf_op | source)
XLA Modules:
  0.0 95.0 jit_solution(17896528200062751198)
XLA Ops:
  1.9 0.7 reshape.20.probe_ref
  2.6 0.0 copy-start.6
  2.6 2.7 %copy.13.key_ref = bf16[1152,576]{1,0:T(8,128)(2,1)} copy(bf16[1152,576]{0,1:T(8,128)(2,1)} %param.11) | data formatting | bytes 2654208 | tf_op args[3]
  5.3 0.0 copy-done.6
  5.3 0.0 copy-start
  5.3 0.0 copy-start.5
  5.3 1.6 %copy.14.value_ref = bf16[1152,576]{1,0:T(8,128)(2,1)} copy(bf16[1152,576]{0,1:T(8,128)(2,1)S(1)} %copy-done.6) | data formatting | bytes 2654208 | tf_op args[4]
  7.0 0.0 copy-done
  7.0 0.0 copy-done.5
  7.0 80.0 %whole.1 = (f32[8,1152]{1,0:T(8,128)S(1)}, bf16[1152,576]{1,0:T(8,128)(2,1)S(1)}, f32[1,576]{1,0:T(1,128)S(1)}, bf16[576,1152]{1,0:T(8,128)(2,1)S(1)}, bf16[576,1152]{1,0:T(8,128)(2,1)S(1)}) custom-call(f32[1]{0:T(128)S(6)} %copy.19.scale_ref, f32[1]{0:T(128)S(6)} %copy.20.bias_ref, bf16[2048,1152]{1,0:T(8,128)(2,1)} %bitcast.3, ...), custom_call_target="tpu_custom_call" | custom-call | tf_op jit(solution)/shard_map/whole/pallas_call | solution.py:513
  87.0 0.0 copy-start.1
  87.0 1.1 %copy-done.1 = bf16[576,1152]{1,0:T(8,128)(2,1)} copy-done((bf16[576,1152]{1,0:T(8,128)(2,1)}, bf16[576,1152]{1,0:T(8,128)(2,1)S(1)}, u32[]{:S(2)}) %copy-start.1) | copy-done | bytes 1327128
  88.1 0.0 copy-start.3
  88.1 1.1 %copy-done.3 = bf16[576,1152]{1,0:T(8,128)(2,1)} copy-done((bf16[576,1152]{1,0:T(8,128)(2,1)}, bf16[576,1152]{1,0:T(8,128)(2,1)S(1)}, u32[]{:S(2)}) %copy-start.3) | copy-done | bytes 1327128
  89.1 0.6 reduce
  89.7 0.0 copy-start.4
  89.7 1.7 %copy.15 = bf16[1152,576]{0,1:T(8,128)(2,1)} copy(bf16[1152,576]{1,0:T(8,128)(2,1)S(1)} %get-tuple-element.17) | data formatting | bytes 2654208
  91.5 0.6 copy.21
  92.1 0.0 copy-done.4
  92.1 0.0 copy-start.2
  92.1 1.1 %copy.22 = bf16[1152,576]{0,1:T(8,128)(2,1)} copy(bf16[1152,576]{0,1:T(8,128)(2,1)S(1)} %bitcast.2) | data formatting | bytes 2654208
  93.2 0.7 copy-done.2
  93.9 1.1 %copy.23 = bf16[576,1152]{1,0:T(8,128)(2,1)} copy(bf16[576,1152]{1,0:T(8,128)(2,1)S(1)} %copy-done.2) | data formatting | bytes 2654208
Async XLA Ops:
  2.6 2.7 %copy-start.6 = (bf16[1152,576]{0,1:T(8,128)(2,1)S(1)}, bf16[1152,576]{0,1:T(8,128)(2,1)}, u32[]{:S(2)}) copy-start(bf16[1152,576]{0,1:T(8,128)(2,1)} %param.12) | copy-start | bytes 3981316
  5.3 1.7 %copy-start = (bf16[576,1152]{1,0:T(8,128)(2,1)S(1)}, bf16[576,1152]{1,0:T(8,128)(2,1)}, u32[]{:S(2)}) copy-start(bf16[576,1152]{1,0:T(8,128)(2,1)} %out_ref.1) | copy-start | bytes 3981316
  5.3 1.7 %copy-start.5 = (bf16[8,1152]{1,0:T(8,128)(2,1)S(1)}, bf16[8,1152]{1,0:T(8,128)(2,1)}, u32[]{:S(2)}) copy-start(bf16[8,1152]{1,0:T(8,128)(2,1)} %captions_ref.1) | copy-start | bytes 55300
  87.0 1.1 %copy-start.1 = (bf16[576,1152]{1,0:T(8,128)(2,1)}, bf16[576,1152]{1,0:T(8,128)(2,1)S(1)}, u32[]{:S(2)}) copy-start(bf16[576,1152]{1,0:T(8,128)(2,1)S(1)} %get-tuple-element.29) | copy-start | bytes 3981316
  88.1 1.1 %copy-start.3 = (bf16[576,1152]{1,0:T(8,128)(2,1)}, bf16[576,1152]{1,0:T(8,128)(2,1)S(1)}, u32[]{:S(2)}) copy-start(bf16[576,1152]{1,0:T(8,128)(2,1)S(1)} %get-tuple-element.13) | copy-start | bytes 3981316
  89.7 2.4 %copy-start.4 = (bf16[576,1152]{1,0:T(8,128)(2,1)S(1)}, bf16[576,1152]{1,0:T(8,128)(2,1)}, u32[]{:S(2)}) copy-start(bf16[576,1152]{1,0:T(8,128)(2,1)} %copy-done.3) | copy-start | bytes 3981316
  92.1 1.8 %copy-start.2 = (bf16[576,1152]{1,0:T(8,128)(2,1)S(1)}, bf16[576,1152]{1,0:T(8,128)(2,1)}, u32[]{:S(2)}) copy-start(bf16[576,1152]{1,0:T(8,128)(2,1)} %copy-done.1) | copy-start | bytes 3981316

commit v3 on v2

v3 whole, which is shorter than its diff:
```python
import math

import jax
import jax.numpy as jnp
from jax import lax
from jax.experimental import pallas as pl
from jax.experimental.pallas import tpu as pltpu
from jax.sharding import PartitionSpec as P

D = 1152
HEADS = 8
HEAD_DIM = 72
PATCHES = 256
IMG_DEV = 8
ROWS = HEADS * HEAD_DIM
FLAT = IMG_DEV * PATCHES
CHUNK = 512
VALUE_AT = 640

MESH = pl.DeviceIdType.MESH
HALF = 162
HALF_ROWS = 288
PART = 41
PIECE = 11
LIST = 168
OWNED = 2
OWNERS = 6
SLOTS = 14
SMALL_AT = 12
WIDE = 1792
SMALL_TILES = WIDE // 256

norm_epsilon = 1e-06


def normalize(rows):
    length = jnp.sqrt(jnp.sum(rows * rows, axis=-1, keepdims=True) + norm_epsilon)
    return (rows / length, length)


def dot(left, right, left_dim=1, right_dim=0, precision=None):
    dims = (((left_dim,), (right_dim,)), ((), ()))
    return lax.dot_general(left, right, dims, precision=precision, preferred_element_type=jnp.float32)


def split_low(values):
    high = values.astype(jnp.bfloat16).astype(jnp.float32)
    return jnp.concatenate([high, values - high], axis=0).astype(jnp.bfloat16)


def head_mask():
    head = lax.broadcasted_iota(jnp.int32, (HEADS, ROWS), 0) * HEAD_DIM
    column = lax.broadcasted_iota(jnp.int32, (HEADS, ROWS), 1)
    return (column >= head) & (column < head + HEAD_DIM)


def probe_rows(probe_ref, own_head):
    row = probe_ref[...].astype(jnp.float32).reshape(1, ROWS)
    return jnp.where(own_head, jnp.broadcast_to(row, (HEADS, ROWS)), 0.0)


def whole_kernel(
    scale_ref,
    bias_ref,
    patches_ref,
    captions_ref,
    probe_ref,
    key_ref,
    value_ref,
    out_ref,
    caption_out,
    probe_out,
    small_slots,
    value_final,
    out_final,
    x_all,
    captions,
    probe_row,
    weights,
    out_weight,
    keys,
    values,
    scores,
    attention,
    units,
    backs,
    backs_got,
    turned,
    rows_wide,
    rows_own,
    away_rows,
    home_rows,
    score_rows,
    small_own,
    value_send,
    value_got,
    value_own,
    rows_all,
    rows_got,
    small_got,
    small_pair,
    small_all,
    pools,
    out_own,
    first_send,
    first_got,
    value_grid,
    value_second,
    value_total,
    value_third,
    value_owned,
    value_all,
    small_owned,
    out_grid,
    out_second,
    out_total,
    out_third,
    out_owned,
    out_all,
    load_sem,
    unit_sem,
    visit_sem,
    pair_sem,
    rows_sem,
    small_sem,
    first_sem,
    value_second_sem,
    value_third_sem,
    value_back_sem,
    small_back_sem,
    value_spread_sem,
    small_spread_sem,
    value_home_sem,
    value_cross_sem,
    out_second_sem,
    out_third_sem,
    out_back_sem,
    out_spread_sem,
    out_home_sem,
    out_cross_sem,
):
    f32, bf16 = jnp.float32, jnp.bfloat16
    highest = lax.Precision.HIGHEST
    me = lax.axis_index("dp")
    core, x, y, z = me % 2, (me // 2) % 4, (me // 8) % 4, me // 32
    first = x + (y - x) * core
    second = y + (x - y) * core

    def device_at(at_z, at_first, at_second, at_core):
        at_x = at_first + (at_second - at_first) * core
        at_y = at_second + (at_first - at_second) * core
        return ((at_z * 4 + at_y) * 4 + at_x) * 2 + at_core

    other = device_at(z, first, second, 1 - core)

    def first_peer(step):
        place = (first + step) % 4
        return device_at(z, place, second, core), place

    def second_peer(step):
        place = (second + step) % 4
        return device_at(z, first, place, core), place

    def third_peer(step):
        place = (z + step) % 8
        return device_at(place, first, second, core), place

    peers = [other]
    peers += [first_peer(step)[0] for step in (1, 2, 3)]
    peers += [second_peer(step)[0] for step in (1, 2, 3)]
    peers += [third_peer(step)[0] for step in range(1, 8)]
    peers += [(me + step) % 256 for step in (1, 2, 254, 255)]
    barrier = pltpu.get_barrier_semaphore()
    for peer in peers:
        pl.semaphore_signal(barrier, inc=1, device_id=(peer,), device_id_type=MESH)

    def load(source, target, slot):
        return pltpu.make_async_copy(source, target, load_sem.at[slot])

    def load_rows(slot):
        part = pl.ds(pl.multiple_of(slot * CHUNK, CHUNK), CHUNK)
        return load(patches_ref.at[part], x_all.at[part], slot)

    load(key_ref, weights.at[0:ROWS], 4).start()
    load(value_ref, weights.at[VALUE_AT : VALUE_AT + ROWS], 5).start()
    for slot in range(4):
        load_rows(slot).start()
    load(probe_ref, probe_row, 8).start()
    load(captions_ref, captions, 7).start()
    load(out_ref, out_weight, 6).start()
    weights[ROWS:VALUE_AT, :] = jnp.zeros((VALUE_AT - ROWS, D), bf16)

    sent = []

    def copy_to(device, source, target, sems, slot):
        return pltpu.make_async_remote_copy(
            src_ref=source,
            dst_ref=target,
            send_sem=sems.at[0, slot],
            recv_sem=sems.at[1, slot],
            device_id=(device,),
            device_id_type=MESH,
        )

    def send(*where):
        copy = copy_to(*where)
        copy.start()
        sent.append(copy)
        return copy

    own_head = head_mask()
    load(probe_ref, probe_row, 8).wait()
    probe = probe_rows(probe_row, own_head)
    probe_out[...] = probe
    probe_low = probe.astype(bf16)

    def project(step, unused):
        load_rows(step).wait()
        part = pl.ds(pl.multiple_of(step * CHUNK, CHUNK), CHUNK)
        both = dot(x_all[part, :], weights[...], 1, 1)
        key_rows = both[:, :ROWS].astype(bf16)
        keys[part, :] = key_rows
        values[part, :] = both[:, VALUE_AT:].astype(bf16)
        score = dot(probe_low, key_rows, 1, 1)
        at = pl.multiple_of(step * 16, 16)
        scores[pl.ds(at, 8), :] = score[:, :PATCHES]
        scores[pl.ds(at + 8, 8), :] = score[:, PATCHES:]
        return unused

    load(key_ref, weights.at[0:ROWS], 4).wait()
    load(value_ref, weights.at[VALUE_AT : VALUE_AT + ROWS], 5).wait()
    lax.fori_loop(0, 3, project, 0)
    load(captions_ref, captions, 7).wait()
    own_unit, own_length = normalize(captions[...].astype(f32))
    units[0] = own_unit
    pl.semaphore_wait(barrier, len(peers))
    unit_copies = [
        send((me + step) % 256, units.at[0], units.at[step], unit_sem, step - 1) for step in (1, 2)
    ]
    lax.fori_loop(3, 4, project, 0)

    score = scores[...] * (1.0 / math.sqrt(HEAD_DIM))
    raised = jnp.exp(score - jnp.max(score, axis=-1, keepdims=True))
    attend = raised / jnp.sum(raised, axis=-1, keepdims=True)
    attention[...] = attend
    pooled = []
    for image in range(IMG_DEV):
        weights = attend[image * 8 : image * 8 + 8].astype(bf16)
        mixed = dot(weights, values[image * PATCHES : (image + 1) * PATCHES, :])
        pooled.append(jnp.sum(jnp.where(own_head, mixed, 0.0), axis=0, keepdims=True))
    pooled = jnp.concatenate(pooled, axis=0)
    load(out_ref, out_weight, 6).wait()
    embedding = dot(pooled.astype(bf16), out_weight[...])
    image_unit, image_length = normalize(embedding)

    for copy in unit_copies:
        copy.wait_recv()
    caption_units = units[...].reshape(24, D)
    scale, bias = scale_ref[0], bias_ref[0]
    logits = scale * dot(image_unit, caption_units, 1, 1, highest) + bias
    same = lax.broadcasted_iota(jnp.int32, (8, 24), 0) == lax.broadcasted_iota(jnp.int32, (8, 24), 1)
    slope = jax.nn.sigmoid(logits) - jnp.where(same, 1.0, 0.0)
    image_total = scale * dot(slope, caption_units, 1, 0, highest)
    embedding_grad = (
        image_total - image_unit * jnp.sum(image_unit * image_total, axis=-1, keepdims=True)
    ) / image_length
    rows_wide[...] = jnp.zeros((16, D), f32)
    rows_wide[0:8, :] = embedding_grad
    rows_wide[8:16, 0:ROWS] = pooled
    rows_own[...] = rows_wide[...].astype(bf16)
    rows_copy = send(other, rows_own, rows_got, rows_sem, 0)
    backs[...] = (scale * dot(slope, image_unit, 0, 0, highest)).reshape(3, 8, D)
    visit_copies = [
        send((me + 256 - step) % 256, backs.at[step], backs_got.at[step - 1], visit_sem, step - 1)
        for step in (1, 2)
    ]

    grad_low = embedding_grad.astype(bf16)
    pooled_grad = dot(grad_low, out_weight[...], 1, 1)
    turned[...] = dot(out_weight[...], grad_low, 1, 1)
    attention_grad = []
    for image in range(IMG_DEV):
        spread_grad = jnp.where(
            own_head, jnp.broadcast_to(pooled_grad[image : image + 1], (HEADS, ROWS)), 0.0
        )
        both = dot(split_low(spread_grad), values[image * PATCHES : (image + 1) * PATCHES, :], 1, 1)
        attention_grad.append(both[0:8] + both[8:16])
    attention_grad = jnp.concatenate(attention_grad, axis=0)
    score_grad = attend * (
        attention_grad - jnp.sum(attend * attention_grad, axis=-1, keepdims=True)
    )

    rows_copy.wait_recv()
    rows_all[0, 0] = rows_own[...]
    rows_all[0, 1] = rows_got[...]
    row_gathers = [
        send(first_peer(step)[0], rows_all.at[0], rows_all.at[step], rows_sem, step)
        for step in (2, 1, 3)
    ]

    def value_rows_grad(start, target):
        for image in range(IMG_DEV):
            for pair in range(2):
                parts = []
                for place in (2 * pair, 2 * pair + 1):
                    at = start + place
                    grads = turned[pl.ds(pl.multiple_of(at * HEAD_DIM, 8), HEAD_DIM), image : image + 1]
                    parts.append(grads * attention[pl.ds(image * 8 + at, 1), :])
                target[pair * 144 : pair * 144 + 144, image * PATCHES : (image + 1) * PATCHES] = (
                    jnp.concatenate(parts, axis=0).astype(bf16)
                )

    value_rows_grad((1 - core) * 4, away_rows)
    for image in range(IMG_DEV):
        part = score_grad[image * 8 : image * 8 + 8]
        lanes = slice(image * PATCHES, (image + 1) * PATCHES)
        away_rows[HALF_ROWS : HALF_ROWS + 16, lanes] = jnp.concatenate(
            [part, jnp.zeros((8, PATCHES), f32)], axis=0
        ).astype(bf16)
        score_rows[:, lanes] = split_low(part)

    value_send[HALF:] = jnp.zeros((LIST - HALF, 16, 128), bf16)
    pair_copies = []
    for block in range(5):
        lanes = slice(block * 256, min(block * 256 + 256, D))
        term = dot(away_rows[...], x_all[:, lanes])
        for tile in range(block * 36, min(block * 36 + 36, HALF)):
            row, lane = tile % 18 * 16, tile // 18 * 128 - block * 256
            value_send[tile] = term[row : row + 16, lane : lane + 128].astype(bf16)
        small_own[:, lanes] = term[HALF_ROWS : HALF_ROWS + 8]
        if block > 0:
            start = (block - 1) * PART
            part = slice(start, start + PART if block < 4 else LIST)
            pair_copies.append(
                send(other, value_send.at[part], value_got.at[part], pair_sem, block - 1)
            )
    probe_part = dot(score_rows[...], keys[...])
    probe_part = jnp.where(own_head, probe_part[0:8] + probe_part[8:16], 0.0) * (1.0 / math.sqrt(HEAD_DIM))
    small_own[:, D:WIDE] = jnp.zeros((8, WIDE - D), f32)
    small_own[:, D : D + ROWS] = probe_part
    small_copy = send(other, small_own, small_got, small_sem, 0)

    for copy in row_gathers:
        copy.wait_recv()
    rows = rows_all[...].astype(f32).reshape(8, 16, D)
    embedding_grads = rows[:, :8].reshape(64, D).astype(bf16)
    pools[...] = rows[:, 8:, :ROWS].reshape(64, ROWS).T
    for block in range(3):
        at = pl.multiple_of(core * HALF_ROWS + block * 96, 32)
        term = dot(pools[pl.ds(at, 96), :].astype(bf16), embedding_grads)
        for row in range(6):
            for lane in range(9):
                out_own[lane * 18 + block * 6 + row] = term[
                    row * 16 : row * 16 + 16, lane * 128 : lane * 128 + 128
                ]
    out_own[HALF:] = jnp.zeros((LIST - HALF, 16, 128), f32)

    def piece_at(place, piece):
        return pl.ds(place * PART + piece * PIECE, PIECE)

    for piece in range(4):
        out_grid[piece] = out_own[piece_at(first, piece)]
    out_copies = []
    for step in (2, 1, 3):
        device, place = second_peer(step)
        out_copies.append(
            send(device, out_grid.at[place], out_second.at[step - 1], out_second_sem, step - 1)
        )

    value_rows_grad(core * 4, home_rows)
    for block in range(5):
        lanes = slice(block * 256, min(block * 256 + 256, D))
        term = dot(home_rows[...], x_all[:, lanes])
        for tile in range(block * 36, min(block * 36 + 36, HALF)):
            row, lane = tile % 18 * 16, tile // 18 * 128 - block * 256
            value_own[tile] = term[row : row + 16, lane : lane + 128]
    value_own[HALF:] = jnp.zeros((LIST - HALF, 16, 128), f32)

    small_copy.wait_recv()
    small_pair[...] = small_own[...] + small_got[...]
    small_gathers = [
        send(first_peer(step)[0], small_pair, small_all.at[step - 1], small_sem, step)
        for step in (2, 1, 3)
    ]
    for copy in pair_copies:
        copy.wait_recv()
    first_copies = []
    for ahead in (2, 1, 3, 0):
        piece = (second + ahead) % 4
        copies = []
        for step in (2, 1, 3):
            device, place = first_peer(step)
            slot = ahead * 3 + step - 1
            part = piece_at(place, piece)
            first_send[slot] = (value_own[part] + value_got[part].astype(f32)).astype(bf16)
            copies.append(send(device, first_send.at[slot], first_got.at[slot], first_sem, slot))
        first_copies.append((ahead, copies))

    def z_order():
        return (4, 3, 5, 2, 6, 1, 7)

    def send_third(total, got, sems):
        return [
            send(
                third_peer(step)[0],
                total.at[pl.ds(third_peer(step)[1] * OWNED, OWNED)],
                got.at[step - 1],
                sems,
                step - 1,
            )
            for step in z_order()
        ]

    for copy in out_copies:
        copy.wait_recv()
    out_total[0:PIECE] = out_grid[second] + out_second[0] + out_second[1] + out_second[2]
    out_total[PIECE:] = jnp.zeros((16 - PIECE, 16, 128), f32)
    out_thirds = send_third(out_total, out_third, out_third_sem)

    for copy in small_gathers:
        copy.wait_recv()
    small = small_pair[...] + small_all[0] + small_all[1] + small_all[2]
    value_grid[:, PIECE:] = jnp.zeros((4, SLOTS - PIECE, 16, 128), f32)
    for tile in range(SMALL_TILES):
        at = (tile // 2, SMALL_AT + tile % 2)
        value_grid[at[0], at[1], 0:8] = small[:, tile * 256 : tile * 256 + 128]
        value_grid[at[0], at[1], 8:16] = small[:, tile * 256 + 128 : tile * 256 + 256]
    value_copies = []
    for ahead, copies in first_copies:
        for copy in copies:
            copy.wait_recv()
        device, piece = second_peer(ahead)
        part = piece_at(first, piece)
        term = value_own[part] + value_got[part].astype(f32)
        for step in (1, 2, 3):
            term = term + first_got[ahead * 3 + step - 1].astype(f32)
        value_grid[piece, 0:PIECE] = term
        if ahead > 0:
            value_copies.append(
                send(device, value_grid.at[piece], value_second.at[ahead - 1], value_second_sem, ahead - 1)
            )

    def send_back(total, got, copies, owned, every, sems):
        for copy in copies:
            copy.wait_recv()
        mine = pl.ds(z * OWNED, OWNED)
        result = total[mine]
        for slot in range(7):
            result = result + got[slot]
        owned[...] = result.astype(bf16)
        every[mine] = result.astype(bf16)

        @pl.when(z < OWNERS)
        def _():
            for step in z_order():
                copy_to(third_peer(step)[0], owned, every.at[mine], sems, step - 1).start()

        return result

    def end_back(owned, every, sems):
        for step in z_order():
            device = third_peer(step)[0]
            source = (z + 8 - step) % 8

            @pl.when(source < OWNERS)
            def _():
                arrived = every.at[pl.ds(source * OWNED, OWNED)]
                copy_to(device, owned, arrived, sems, step - 1).wait_recv()

            @pl.when(z < OWNERS)
            def _():
                copy_to(device, owned, every.at[pl.ds(z * OWNED, OWNED)], sems, step - 1).wait_send()

    def send_home(part, final, sems, ahead):
        piece = final.at[core, first, part]
        return [
            send(first_peer(step)[0], piece, piece, sems, ahead * 3 + step - 1) for step in (2, 1, 3)
        ]

    def send_spread(every, final, spread_sems, home_sems):
        final[core, first, second] = every[0:PIECE]
        piece = final.at[core, first, second]
        spread = [
            send(second_peer(step)[0], every.at[0:PIECE], piece, spread_sems, step - 1)
            for step in (2, 1, 3)
        ]
        return spread, send_home(second, final, home_sems, 0)

    def forward_spread(spread, final, home_sems):
        homes = []
        for copy, step in zip(spread[1:] + spread[:1], (1, 3, 2)):
            copy.wait_recv()
            homes += send_home((second + 4 - step) % 4, final, home_sems, step)
        return homes

    def forward_homes(homes, final, cross_sems):
        mine = final.at[core, first]
        cross = [send(other, mine, mine, cross_sems, 0)]
        for place, step in ((1, 1), (2, 3), (0, 2)):
            for copy in homes[place::3]:
                copy.wait_recv()
            part = final.at[core, (first + 4 - step) % 4]
            cross.append(send(other, part, part, cross_sems, step))
        return cross

    send_back(out_total, out_third, out_thirds, out_owned, out_all, out_back_sem)

    for copy in value_copies:
        copy.wait_recv()
    value_total[0:SLOTS] = value_grid[second] + value_second[0] + value_second[1] + value_second[2]
    value_total[SLOTS:] = jnp.zeros((16 - SLOTS, 16, 128), f32)
    value_thirds = send_third(value_total, value_third, value_third_sem)

    end_back(out_owned, out_all, out_back_sem)
    out_spread, out_homes = send_spread(out_all, out_final, out_spread_sem, out_home_sem)

    small_sum = send_back(
        value_total, value_third, value_thirds, value_owned, value_all, value_back_sem
    )
    small_owned[...] = small_sum
    mine = small_slots.at[second]

    @pl.when(z == OWNERS)
    def _():
        small_slots[second] = small_sum
        for step in z_order():
            copy_to(third_peer(step)[0], small_owned, mine, small_back_sem, step - 1).start()
        for step in z_order():
            copy_to(third_peer(step)[0], small_owned, mine, small_back_sem, step - 1).wait_send()

    out_homes += forward_spread(out_spread, out_final, out_home_sem)

    end_back(value_owned, value_all, value_back_sem)
    value_spread, value_homes = send_spread(value_all, value_final, value_spread_sem, value_home_sem)

    @pl.when(z != OWNERS)
    def _():
        step = (z + 8 - OWNERS) % 8
        copy_to(third_peer(step)[0], small_owned, mine, small_back_sem, step - 1).wait_recv()

    small_spread = [
        send(second_peer(step)[0], mine, mine, small_spread_sem, step - 1) for step in (2, 1, 3)
    ]
    value_homes += forward_spread(value_spread, value_final, value_home_sem)
    cross = forward_homes(out_homes, out_final, out_cross_sem)

    for copy in visit_copies:
        copy.wait_recv()
    caption_total = backs[0] + backs_got[0] + backs_got[1]
    caption_out[...] = (
        caption_total - own_unit * jnp.sum(own_unit * caption_total, axis=-1, keepdims=True)
    ) / own_length

    cross += forward_homes(value_homes, value_final, value_cross_sem)
    for copy in small_spread + cross:
        copy.wait_recv()
    for copy in sent:
        copy.wait_send()


def finish_kernel(
    probe_ref,
    caption_ref,
    small_ref,
    value_ref,
    out_ref,
    caption_out,
    probe_out,
    key_out,
    value_out,
    out_out,
    key_rows,
    value_rows,
    out_rows,
    store_sem,
):
    f32, bf16 = jnp.float32, jnp.bfloat16

    def store(source, target, slot):
        return pltpu.make_async_copy(source, target, store_sem.at[slot])

    stores = [store(caption_ref, caption_out, 0)]
    stores[0].start()

    def unpack(source, target, sink, slot):
        for core in range(2):
            for tile in range(HALF):
                place, at = tile // PART, tile % PART
                row = core * HALF_ROWS + tile % 18 * 16
                lane = tile // 18 * 128
                target[row : row + 16, lane : lane + 128] = source[core, place, at // PIECE, at % PIECE]
        stores.append(store(target, sink, slot))
        stores[-1].start()

    unpack(value_ref, value_rows, value_out, 1)
    unpack(out_ref, out_rows, out_out, 2)
    small = []
    for tile in range(SMALL_TILES):
        both = small_ref[tile // 2, tile % 2]
        small += [both[0:8], both[8:16]]
    probe_out[...] = jnp.sum(jnp.concatenate(small[9:], axis=1)[:, :ROWS], axis=0, keepdims=True)
    patch_sum = jnp.concatenate(small[:9], axis=1) * (1.0 / math.sqrt(HEAD_DIM))
    probe = probe_ref[...].T
    for pair in range(4):
        parts = []
        for head in (2 * pair, 2 * pair + 1):
            column = probe[head * HEAD_DIM : head * HEAD_DIM + HEAD_DIM, head : head + 1]
            parts.append(column * patch_sum[head : head + 1])
        key_rows[pair * 144 : pair * 144 + 144, :] = jnp.concatenate(parts, axis=0).astype(bf16)
    stores.append(store(key_rows, key_out, 3))
    stores[-1].start()
    for copy in stores:
        copy.wait()


def in_hbm(array):
    return pltpu.with_memory_space_constraint(array, pltpu.HBM)


def on_device(
    patches, captions, probe_query, key_weight, value_weight, out_weight, logit_scale, logit_bias
):
    f32, bf16 = jnp.float32, jnp.bfloat16
    vmem = pl.BlockSpec(memory_space=pltpu.VMEM)
    smem = pl.BlockSpec(memory_space=pltpu.SMEM)
    hbm = pl.BlockSpec(memory_space=pltpu.HBM)
    dma = pltpu.SemaphoreType.DMA
    caption_grad, probe, small, value_final, out_final = pl.pallas_call(
        whole_kernel,
        out_shape=(
            jax.ShapeDtypeStruct((IMG_DEV, D), f32),
            jax.ShapeDtypeStruct((HEADS, ROWS), f32),
            jax.ShapeDtypeStruct((4, OWNED, 16, 128), f32),
            jax.ShapeDtypeStruct((2, 4, 4, PIECE, 16, 128), bf16),
            jax.ShapeDtypeStruct((2, 4, 4, PIECE, 16, 128), bf16),
        ),
        in_specs=[smem, smem, hbm, hbm, hbm, hbm, hbm, hbm],
        out_specs=[vmem] * 5,
        scratch_shapes=[
            pltpu.VMEM((FLAT, D), bf16),
            pltpu.VMEM((IMG_DEV, D), bf16),
            pltpu.VMEM((ROWS,), bf16),
            pltpu.VMEM((VALUE_AT + ROWS, D), bf16),
            pltpu.VMEM((ROWS, D), bf16),
            pltpu.VMEM((FLAT, ROWS), bf16),
            pltpu.VMEM((FLAT, ROWS), bf16),
            pltpu.VMEM((64, PATCHES), f32),
            pltpu.VMEM((64, PATCHES), f32),
            pltpu.VMEM((3, 8, D), f32),
            pltpu.VMEM((3, 8, D), f32),
            pltpu.VMEM((2, 8, D), f32),
            pltpu.VMEM((ROWS, 8), f32),
            pltpu.VMEM((16, D), f32),
            pltpu.VMEM((16, D), bf16),
            pltpu.VMEM((HALF_ROWS + 16, FLAT), bf16),
            pltpu.VMEM((HALF_ROWS, FLAT), bf16),
            pltpu.VMEM((16, FLAT), bf16),
            pltpu.VMEM((8, WIDE), f32),
            pltpu.VMEM((LIST, 16, 128), bf16),
            pltpu.VMEM((LIST, 16, 128), bf16),
            pltpu.VMEM((LIST, 16, 128), f32),
            pltpu.VMEM((4, 2, 16, D), bf16),
            pltpu.VMEM((16, D), bf16),
            pltpu.VMEM((8, WIDE), f32),
            pltpu.VMEM((8, WIDE), f32),
            pltpu.VMEM((3, 8, WIDE), f32),
            pltpu.VMEM((ROWS, 64), f32),
            pltpu.VMEM((LIST, 16, 128), f32),
            pltpu.VMEM((12, PIECE, 16, 128), bf16),
            pltpu.VMEM((12, PIECE, 16, 128), bf16),
            pltpu.VMEM((4, SLOTS, 16, 128), f32),
            pltpu.VMEM((3, SLOTS, 16, 128), f32),
            pltpu.VMEM((16, 16, 128), f32),
            pltpu.VMEM((7, OWNED, 16, 128), f32),
            pltpu.VMEM((OWNED, 16, 128), bf16),
            pltpu.VMEM((16, 16, 128), bf16),
            pltpu.VMEM((OWNED, 16, 128), f32),
            pltpu.VMEM((4, PIECE, 16, 128), f32),
            pltpu.VMEM((3, PIECE, 16, 128), f32),
            pltpu.VMEM((16, 16, 128), f32),
            pltpu.VMEM((7, OWNED, 16, 128), f32),
            pltpu.VMEM((OWNED, 16, 128), bf16),
            pltpu.VMEM((16, 16, 128), bf16),
            dma((9,)),
            dma((2, 2)),
            dma((2, 2)),
            dma((2, 4)),
            dma((2, 4)),
            dma((2, 4)),
            dma((2, 12)),
            dma((2, 3)),
            dma((2, 7)),
            dma((2, 7)),
            dma((2, 7)),
            dma((2, 3)),
            dma((2, 3)),
            dma((2, 12)),
            dma((2, 4)),
            dma((2, 3)),
            dma((2, 7)),
            dma((2, 7)),
            dma((2, 3)),
            dma((2, 12)),
            dma((2, 4)),
        ],
        compiler_params=pltpu.CompilerParams(
            collective_id=0, has_side_effects=True, vmem_limit_bytes=40 * 1024 * 1024
        ),
        name="whole",
    )(
        logit_scale,
        logit_bias,
        in_hbm(patches.reshape(FLAT, D)),
        in_hbm(captions),
        in_hbm(probe_query),
        in_hbm(key_weight.T),
        in_hbm(value_weight.T),
        in_hbm(out_weight),
    )
    caption_grad, probe_grad, key_turned, value_turned, out_grad = pl.pallas_call(
        finish_kernel,
        out_shape=(
            jax.ShapeDtypeStruct((IMG_DEV, D), f32),
            jax.ShapeDtypeStruct((1, ROWS), f32),
            jax.ShapeDtypeStruct((ROWS, D), bf16),
            jax.ShapeDtypeStruct((ROWS, D), bf16),
            jax.ShapeDtypeStruct((ROWS, D), bf16),
        ),
        in_specs=[vmem] * 5,
        out_specs=[hbm, vmem, hbm, hbm, hbm],
        scratch_shapes=[
            pltpu.VMEM((ROWS, D), bf16),
            pltpu.VMEM((ROWS, D), bf16),
            pltpu.VMEM((ROWS, D), bf16),
            dma((4,)),
        ],
        compiler_params=pltpu.CompilerParams(vmem_limit_bytes=16 * 1024 * 1024),
        name="finish",
    )(probe, caption_grad, small, value_final, out_final)
    return (caption_grad, probe_grad.reshape(ROWS), key_turned.T, value_turned.T, out_grad)


def solution(mesh):
    placed = (P("dp", None, None), P("dp", None), P(), P(), P(), P(), P(), P())
    return jax.shard_map(
        on_device,
        mesh=mesh,
        in_specs=placed,
        out_specs=(P("dp", None), P(), P(), P(), P()),
        check_vma=False,
    )
```

time: 95.2 us -> 75.1 us (0.79)
  local copies, waits for them, and re-layouts: 12.4 us -> 0 us
  Pallas kernels: 80 us -> 72.5 us
    unnamed x20 -> x0, local copies, waits for them, and re-layouts: 11.7 us -> none
    pallas_call x1, Pallas kernels: 80 us -> 70 us  [on_device(): pl.pallas_call(whole_kernel, out_shape=(jax.ShapeDtypeStruct((IMG_DEV, D)...]
    pallas_call x0 -> x1, Pallas kernels: none -> 2.5 us  [on_device(): pl.pallas_call(finish_kernel, out_shape=(jax.ShapeDtypeStruct((IMG_DEV, D...]
where the time goes in v3:
time: 75.1 us; the launch traced here: 75 us
  Pallas kernels  72.5 us (97%)
  between operations  1.94 us (3%)
    pallas_call x1, Pallas kernels, on_device(): pl.pallas_call(whole_kernel, out_shape=(jax.ShapeDtypeStruct((IMG_DEV, D)...  70 us
    pallas_call x1, Pallas kernels, on_device(): pl.pallas_call(finish_kernel, out_shape=(jax.ShapeDtypeStruct((IMG_DEV, D...  2.5 us

profile of v3, /device:TPU:1, one launch (start us, length us, event | category | flops | bytes accessed | tf_op | source)
XLA Modules:
  0.0 75.0 jit_solution(8682320617700922816)
XLA Ops:
  1.9 70.0 %whole.1 = (f32[8,1152]{1,0:T(8,128)S(1)}, f32[8,576]{1,0:T(8,128)S(1)}, f32[4,2,16,128]{3,2,1,0:T(8,128)S(1)}, bf16[2,4,4,11,16,128]{5,4,3,2,1,0:T(8,128)(2,1)S(1)}, bf16[2,4,4,11,16,128]{5,4,3,2,1,0:T(8,128)(2,1)S(1)}) custom-call(f32[1]{0:T(128)S(6)} %copy.13.scale_ref, f32[1]{0:T(128)S(6)} %copy.14.bias_ref, bf16[2048,1152]{1,0:T(8,128)(2,1)} %bitcast.5, ...), custom_call_target="tpu_custom_call" | custom-call | tf_op jit(solution)/shard_map/whole/pallas_call | solution.py:628
  71.9 2.5 %finish.1 = (f32[8,1152]{1,0:T(8,128)}, f32[1,576]{1,0:T(1,128)S(1)}, bf16[576,1152]{1,0:T(8,128)(2,1)}, bf16[576,1152]{1,0:T(8,128)(2,1)}, bf16[576,1152]{1,0:T(8,128)(2,1)}) custom-call(f32[8,576]{1,0:T(8,128)S(1)} %get-tuple-element.15.probe_ref, f32[8,1152]{1,0:T(8,128)S(1)} %get-tuple-element.16.caption_ref, ...), custom_call_target="tpu_custom_call" | custom-call | tf_op jit(solution)/shard_map/finish/pallas_call | solution.py:720
  74.4 0.6 reduce

commit v4 on v3

v4 whole, which is shorter than its diff:
```python
import math

import jax
import jax.numpy as jnp
from jax import lax
from jax.experimental import pallas as pl
from jax.experimental.pallas import tpu as pltpu
from jax.sharding import PartitionSpec as P

D = 1152
HEADS = 8
HEAD_DIM = 72
PATCHES = 256
IMG_DEV = 8
ROWS = HEADS * HEAD_DIM
FLAT = IMG_DEV * PATCHES
CHUNK = 512
VALUE_AT = 640

MESH = pl.DeviceIdType.MESH
HALF = 162
HALF_ROWS = 288
PART = 41
PIECE = 11
LIST = 168
OWNED = 2
OWNERS = 6
SLOTS = 14
SMALL_AT = 12
WIDE = 1792
SMALL_TILES = WIDE // 256

norm_epsilon = 1e-06


def normalize(rows):
    length = jnp.sqrt(jnp.sum(rows * rows, axis=-1, keepdims=True) + norm_epsilon)
    return (rows / length, length)


def dot(left, right, left_dim=1, right_dim=0, precision=None):
    dims = (((left_dim,), (right_dim,)), ((), ()))
    return lax.dot_general(left, right, dims, precision=precision, preferred_element_type=jnp.float32)


def split_low(values):
    high = values.astype(jnp.bfloat16).astype(jnp.float32)
    return jnp.concatenate([high, values - high], axis=0).astype(jnp.bfloat16)


def head_mask():
    head = lax.broadcasted_iota(jnp.int32, (HEADS, ROWS), 0) * HEAD_DIM
    column = lax.broadcasted_iota(jnp.int32, (HEADS, ROWS), 1)
    return (column >= head) & (column < head + HEAD_DIM)


def probe_rows(probe_ref, own_head):
    row = probe_ref[...].astype(jnp.float32).reshape(1, ROWS)
    return jnp.where(own_head, jnp.broadcast_to(row, (HEADS, ROWS)), 0.0)


def whole_kernel(
    scale_ref,
    bias_ref,
    patches_ref,
    captions_ref,
    probe_ref,
    key_ref,
    value_ref,
    out_ref,
    caption_out,
    probe_out,
    key_out,
    value_out,
    out_out,
    x_all,
    captions,
    probe_row,
    weights,
    out_weight,
    keys,
    values,
    scores,
    attention,
    units,
    backs,
    backs_got,
    turned,
    rows_wide,
    rows_own,
    away_rows,
    home_rows,
    score_rows,
    small_own,
    value_send,
    value_got,
    value_own,
    rows_all,
    rows_got,
    small_got,
    small_pair,
    small_all,
    pools,
    out_own,
    first_send,
    first_got,
    value_grid,
    value_second,
    value_total,
    value_third,
    value_owned,
    value_all,
    small_owned,
    small_slots,
    value_final,
    out_grid,
    out_second,
    out_total,
    out_third,
    out_owned,
    out_all,
    out_final,
    load_sem,
    link_sem,
):
    f32, bf16 = jnp.float32, jnp.bfloat16
    highest = lax.Precision.HIGHEST
    me = lax.axis_index("dp")
    core, x, y, z = me % 2, (me // 2) % 4, (me // 8) % 4, me // 32
    first = x + (y - x) * core
    second = y + (x - y) * core

    def device_at(at_z, at_first, at_second, at_core):
        at_x = at_first + (at_second - at_first) * core
        at_y = at_second + (at_first - at_second) * core
        return ((at_z * 4 + at_y) * 4 + at_x) * 2 + at_core

    other = device_at(z, first, second, 1 - core)

    def first_peer(step):
        place = (first + step) % 4
        return device_at(z, place, second, core), place

    def second_peer(step):
        place = (second + step) % 4
        return device_at(z, first, place, core), place

    def third_peer(step):
        place = (z + step) % 8
        return device_at(place, first, second, core), place

    peers = [other]
    peers += [first_peer(step)[0] for step in (1, 2, 3)]
    peers += [second_peer(step)[0] for step in (1, 2, 3)]
    peers += [third_peer(step)[0] for step in range(1, 8)]
    peers += [(me + step) % 256 for step in (1, 2, 254, 255)]
    barrier = pltpu.get_barrier_semaphore()
    for peer in peers:
        pl.semaphore_signal(barrier, inc=1, device_id=(peer,), device_id_type=MESH)

    def load(source, target, slot):
        return pltpu.make_async_copy(source, target, load_sem.at[slot])

    def load_rows(slot):
        part = pl.ds(pl.multiple_of(slot * CHUNK, CHUNK), CHUNK)
        return load(patches_ref.at[part], x_all.at[part], slot)

    load(probe_ref, probe_row, 8).start()
    load(key_ref, weights.at[0:ROWS], 4).start()
    load(value_ref, weights.at[VALUE_AT : VALUE_AT + ROWS], 5).start()
    load_rows(0).start()
    load(captions_ref, captions, 7).start()
    for slot in (1, 2, 3):
        load_rows(slot).start()
    load(out_ref, out_weight, 6).start()
    weights[ROWS:VALUE_AT, :] = jnp.zeros((VALUE_AT - ROWS, D), bf16)

    used = []
    ends = []

    def new_sem():
        used.append(None)
        return link_sem.at[len(used) - 1]

    def send(device, source, target, leave, arrive):
        pltpu.make_async_remote_copy(
            src_ref=source,
            dst_ref=target,
            send_sem=leave,
            recv_sem=arrive,
            device_id=(device,),
            device_id_type=MESH,
        ).start()

    def wait(bytes_of, sem):
        pltpu.make_async_copy(bytes_of, bytes_of, sem).wait()

    def send_all(copies, bytes_of):
        leave, arrive = new_sem(), new_sem()
        for device, source, target in copies:
            send(device, source, target, leave, arrive)
        ends.append((bytes_of, leave))
        return bytes_of, arrive

    own_head = head_mask()
    load(probe_ref, probe_row, 8).wait()
    probe = probe_rows(probe_row, own_head)
    probe_low = probe.astype(bf16)

    def project(step, unused):
        load_rows(step).wait()
        part = pl.ds(pl.multiple_of(step * CHUNK, CHUNK), CHUNK)
        both = dot(x_all[part, :], weights[...], 1, 1)
        key_rows = both[:, :ROWS].astype(bf16)
        keys[part, :] = key_rows
        values[part, :] = both[:, VALUE_AT:].astype(bf16)
        score = dot(probe_low, key_rows, 1, 1)
        at = pl.multiple_of(step * 16, 16)
        scores[pl.ds(at, 8), :] = score[:, :PATCHES]
        scores[pl.ds(at + 8, 8), :] = score[:, PATCHES:]
        return unused

    load(key_ref, weights.at[0:ROWS], 4).wait()
    load(value_ref, weights.at[VALUE_AT : VALUE_AT + ROWS], 5).wait()
    lax.fori_loop(0, 3, project, 0)
    load(captions_ref, captions, 7).wait()
    own_unit, own_length = normalize(captions[...].astype(f32))
    units[0] = own_unit
    pl.semaphore_wait(barrier, len(peers))
    unit_copies = send_all(
        [((me + step) % 256, units.at[0], units.at[step]) for step in (1, 2)], units.at[1:3]
    )
    lax.fori_loop(3, 4, project, 0)

    score = scores[...] * (1.0 / math.sqrt(HEAD_DIM))
    raised = jnp.exp(score - jnp.max(score, axis=-1, keepdims=True))
    attend = raised / jnp.sum(raised, axis=-1, keepdims=True)
    attention[...] = attend
    pooled = []
    for image in range(IMG_DEV):
        weights = attend[image * 8 : image * 8 + 8].astype(bf16)
        mixed = dot(weights, values[image * PATCHES : (image + 1) * PATCHES, :])
        pooled.append(jnp.sum(jnp.where(own_head, mixed, 0.0), axis=0, keepdims=True))
    pooled = jnp.concatenate(pooled, axis=0)
    load(out_ref, out_weight, 6).wait()
    embedding = dot(pooled.astype(bf16), out_weight[...])
    image_unit, image_length = normalize(embedding)

    wait(*unit_copies)
    caption_units = units[...].reshape(24, D)
    scale, bias = scale_ref[0], bias_ref[0]
    logits = scale * dot(image_unit, caption_units, 1, 1, highest) + bias
    same = lax.broadcasted_iota(jnp.int32, (8, 24), 0) == lax.broadcasted_iota(jnp.int32, (8, 24), 1)
    slope = jax.nn.sigmoid(logits) - jnp.where(same, 1.0, 0.0)
    image_total = scale * dot(slope, caption_units, 1, 0, highest)
    embedding_grad = (
        image_total - image_unit * jnp.sum(image_unit * image_total, axis=-1, keepdims=True)
    ) / image_length
    rows_wide[...] = jnp.zeros((16, D), f32)
    rows_wide[0:8, :] = embedding_grad
    rows_wide[8:16, 0:ROWS] = pooled
    rows_own[...] = rows_wide[...].astype(bf16)
    rows_copy = send_all([(other, rows_own, rows_got)], rows_got)
    backs[...] = (scale * dot(slope, image_unit, 0, 0, highest)).reshape(3, 8, D)
    visit_copies = send_all(
        [
            ((me + 256 - step) % 256, backs.at[step], backs_got.at[step - 1])
            for step in (1, 2)
        ],
        backs_got,
    )

    grad_low = embedding_grad.astype(bf16)
    pooled_grad = dot(grad_low, out_weight[...], 1, 1)
    turned[...] = dot(out_weight[...], grad_low, 1, 1)
    attention_grad = []
    for image in range(IMG_DEV):
        spread_grad = jnp.where(
            own_head, jnp.broadcast_to(pooled_grad[image : image + 1], (HEADS, ROWS)), 0.0
        )
        both = dot(split_low(spread_grad), values[image * PATCHES : (image + 1) * PATCHES, :], 1, 1)
        attention_grad.append(both[0:8] + both[8:16])
    attention_grad = jnp.concatenate(attention_grad, axis=0)
    score_grad = attend * (
        attention_grad - jnp.sum(attend * attention_grad, axis=-1, keepdims=True)
    )

    wait(*rows_copy)
    rows_all[0, 0] = rows_own[...]
    rows_all[0, 1] = rows_got[...]
    row_gathers = send_all(
        [(first_peer(step)[0], rows_all.at[0], rows_all.at[step]) for step in (2, 1, 3)],
        rows_all.at[1:4],
    )

    def value_rows_grad(start, target):
        for image in range(IMG_DEV):
            for pair in range(2):
                parts = []
                for place in (2 * pair, 2 * pair + 1):
                    at = start + place
                    grads = turned[pl.ds(pl.multiple_of(at * HEAD_DIM, 8), HEAD_DIM), image : image + 1]
                    parts.append(grads * attention[pl.ds(image * 8 + at, 1), :])
                target[pair * 144 : pair * 144 + 144, image * PATCHES : (image + 1) * PATCHES] = (
                    jnp.concatenate(parts, axis=0).astype(bf16)
                )

    value_rows_grad((1 - core) * 4, away_rows)
    for image in range(IMG_DEV):
        part = score_grad[image * 8 : image * 8 + 8]
        lanes = slice(image * PATCHES, (image + 1) * PATCHES)
        away_rows[HALF_ROWS : HALF_ROWS + 16, lanes] = jnp.concatenate(
            [part, jnp.zeros((8, PATCHES), f32)], axis=0
        ).astype(bf16)
        score_rows[:, lanes] = split_low(part)

    value_send[HALF:] = jnp.zeros((LIST - HALF, 16, 128), bf16)
    pair_leave, pair_arrive = new_sem(), new_sem()
    ends.append((value_send, pair_leave))
    for block in range(5):
        lanes = slice(block * 256, min(block * 256 + 256, D))
        term = dot(away_rows[...], x_all[:, lanes])
        for tile in range(block * 36, min(block * 36 + 36, HALF)):
            row, lane = tile % 18 * 16, tile // 18 * 128 - block * 256
            value_send[tile] = term[row : row + 16, lane : lane + 128].astype(bf16)
        small_own[:, lanes] = term[HALF_ROWS : HALF_ROWS + 8]
        if block > 0:
            start = (block - 1) * PART
            part = slice(start, start + PART if block < 4 else LIST)
            send(other, value_send.at[part], value_got.at[part], pair_leave, pair_arrive)
    probe_part = dot(score_rows[...], keys[...])
    probe_part = jnp.where(own_head, probe_part[0:8] + probe_part[8:16], 0.0) * (1.0 / math.sqrt(HEAD_DIM))
    small_own[:, D:WIDE] = jnp.zeros((8, WIDE - D), f32)
    small_own[:, D : D + ROWS] = probe_part
    small_copy = send_all([(other, small_own, small_got)], small_got)

    value_rows_grad(core * 4, home_rows)
    for block in range(5):
        lanes = slice(block * 256, min(block * 256 + 256, D))
        term = dot(home_rows[...], x_all[:, lanes])
        for tile in range(block * 36, min(block * 36 + 36, HALF)):
            row, lane = tile % 18 * 16, tile // 18 * 128 - block * 256
            value_own[tile] = term[row : row + 16, lane : lane + 128]
    value_own[HALF:] = jnp.zeros((LIST - HALF, 16, 128), f32)

    wait(*small_copy)
    small_pair[...] = small_own[...] + small_got[...]
    small_gathers = send_all(
        [(first_peer(step)[0], small_pair, small_all.at[step - 1]) for step in (2, 1, 3)], small_all
    )
    def piece_at(place, piece):
        return pl.ds(place * PART + piece * PIECE, PIECE)

    wait(value_got, pair_arrive)
    first_copies = []
    for ahead in (2, 1, 3, 0):
        piece = (second + ahead) % 4
        copies = []
        for step in (2, 1, 3):
            device, place = first_peer(step)
            slot = ahead * 3 + step - 1
            part = piece_at(place, piece)
            first_send[slot] = (value_own[part] + value_got[part].astype(f32)).astype(bf16)
            copies.append((device, first_send.at[slot], first_got.at[slot]))
        first_copies.append((ahead, send_all(copies, first_got.at[ahead * 3 : ahead * 3 + 3])))

    wait(*row_gathers)
    rows = rows_all[...].astype(f32).reshape(8, 16, D)
    embedding_grads = rows[:, :8].reshape(64, D).astype(bf16)
    pools[...] = rows[:, 8:, :ROWS].reshape(64, ROWS).T
    for block in range(3):
        at = pl.multiple_of(core * HALF_ROWS + block * 96, 32)
        term = dot(pools[pl.ds(at, 96), :].astype(bf16), embedding_grads)
        for row in range(6):
            for lane in range(9):
                out_own[lane * 18 + block * 6 + row] = term[
                    row * 16 : row * 16 + 16, lane * 128 : lane * 128 + 128
                ]
    out_own[HALF:] = jnp.zeros((LIST - HALF, 16, 128), f32)

    for piece in range(4):
        out_grid[piece] = out_own[piece_at(first, piece)]
    out_copies = send_all(
        [
            (second_peer(step)[0], out_grid.at[second_peer(step)[1]], out_second.at[step - 1])
            for step in (2, 1, 3)
        ],
        out_second,
    )

    wait(*small_gathers)
    small = small_pair[...] + small_all[0] + small_all[1] + small_all[2]
    value_grid[:, PIECE:] = jnp.zeros((4, SLOTS - PIECE, 16, 128), f32)
    for tile in range(SMALL_TILES):
        at = (tile // 2, SMALL_AT + tile % 2)
        value_grid[at[0], at[1], 0:8] = small[:, tile * 256 : tile * 256 + 128]
        value_grid[at[0], at[1], 8:16] = small[:, tile * 256 + 128 : tile * 256 + 256]
    value_leave, value_arrive = new_sem(), new_sem()
    for ahead, copies in first_copies:
        wait(*copies)
        device, piece = second_peer(ahead)
        part = piece_at(first, piece)
        term = value_own[part] + value_got[part].astype(f32)
        for step in (1, 2, 3):
            term = term + first_got[ahead * 3 + step - 1].astype(f32)
        value_grid[piece, 0:PIECE] = term
        if ahead > 0:
            send(device, value_grid.at[piece], value_second.at[ahead - 1], value_leave, value_arrive)
    ends.append((value_second, value_leave))

    def z_order():
        return (4, 3, 5, 2, 6, 1, 7)

    def send_third(total, got):
        copies = []
        for step in z_order():
            device, place = third_peer(step)
            copies.append((device, total.at[pl.ds(place * OWNED, OWNED)], got.at[step - 1]))
        return send_all(copies, got)

    def send_back(total, got, copies, owned, every):
        wait(*copies)
        mine = pl.ds(z * OWNED, OWNED)
        result = total[mine]
        for slot in range(7):
            result = result + got[slot]
        owned[...] = result.astype(bf16)
        every[mine] = result.astype(bf16)
        leave, arrive = new_sem(), new_sem()

        @pl.when(z < OWNERS)
        def _():
            for step in z_order():
                send(third_peer(step)[0], owned, every.at[mine], leave, arrive)

        return result, leave, arrive

    def end_back(every, leave, arrive):
        @pl.when(z < OWNERS)
        def _():
            wait(every.at[0 : (OWNERS - 1) * OWNED], arrive)
            wait(every.at[0 : 7 * OWNED], leave)

        @pl.when(z >= OWNERS)
        def _():
            wait(every.at[0 : OWNERS * OWNED], arrive)

    def send_home(part, final, leave, arrives):
        piece = final.at[core, first, part]
        for step in (2, 1, 3):
            send(first_peer(step)[0], piece, piece, leave, arrives[step - 1])

    def send_spread(every, final):
        final[core, first, second] = every[0:PIECE]
        piece = final.at[core, first, second]
        leave, arrives = new_sem(), [new_sem() for _ in range(3)]
        for step in (2, 1, 3):
            send(second_peer(step)[0], every.at[0:PIECE], piece, leave, arrives[step - 1])
        ends.append((final.at[core, first, 0:3], leave))
        home_leave, home_arrives = new_sem(), [new_sem() for _ in range(3)]
        send_home(second, final, home_leave, home_arrives)
        ends.append((final.at[core, 0:3], home_leave))
        return arrives, home_leave, home_arrives

    def forward_spread(final, arrives, home_leave, home_arrives):
        for step in (1, 3, 2):
            place = (second + 4 - step) % 4
            wait(final.at[core, first, place], arrives[step - 1])
            send_home(place, final, home_leave, home_arrives)

    def forward_homes(final, home_arrives):
        leave, arrive = new_sem(), new_sem()
        send(other, final.at[core, first], final.at[core, first], leave, arrive)
        for step in (1, 3, 2):
            part = final.at[core, (first + 4 - step) % 4]
            wait(part, home_arrives[step - 1])
            send(other, part, part, leave, arrive)
        ends.append((final.at[1 - core], leave))
        return arrive

    def unpack(final, which, target):
        for tile in range(HALF):
            place, at = tile // PART, tile % PART
            row = pl.ds(pl.multiple_of(which * HALF_ROWS + tile % 18 * 16, 16), 16)
            lane = tile // 18 * 128
            target[row, lane : lane + 128] = final[which, place, at // PIECE, at % PIECE]

    wait(*out_copies)
    out_total[0:PIECE] = out_grid[second] + out_second[0] + out_second[1] + out_second[2]
    out_total[PIECE:] = jnp.zeros((16 - PIECE, 16, 128), f32)
    out_thirds = send_third(out_total, out_third)

    wait(value_second, value_arrive)
    value_total[0:SLOTS] = value_grid[second] + value_second[0] + value_second[1] + value_second[2]
    value_total[SLOTS:] = jnp.zeros((16 - SLOTS, 16, 128), f32)
    value_thirds = send_third(value_total, value_third)

    _, *out_back = send_back(out_total, out_third, out_thirds, out_owned, out_all)

    small_sum, *value_back = send_back(value_total, value_third, value_thirds, value_owned, value_all)
    small_owned[...] = small_sum
    mine = small_slots.at[second]
    small_leave, small_arrive = new_sem(), new_sem()

    @pl.when(z == OWNERS)
    def _():
        small_slots[second] = small_sum
        for step in z_order():
            send(third_peer(step)[0], small_owned, mine, small_leave, small_arrive)

    end_back(out_all, *out_back)
    out_spread, *out_homes = send_spread(out_all, out_final)

    end_back(value_all, *value_back)
    value_spread, *value_homes = send_spread(value_all, value_final)

    @pl.when(z == OWNERS)
    def _():
        wait(value_total.at[0 : 7 * OWNED], small_leave)

    @pl.when(z != OWNERS)
    def _():
        wait(mine, small_arrive)

    small_spread = send_all(
        [(second_peer(step)[0], mine, mine) for step in (2, 1, 3)], small_slots.at[0:3]
    )
    forward_spread(out_final, out_spread, *out_homes)
    forward_spread(value_final, value_spread, *value_homes)

    wait(*visit_copies)
    caption_total = backs[0] + backs_got[0] + backs_got[1]
    caption_out[...] = (
        caption_total - own_unit * jnp.sum(own_unit * caption_total, axis=-1, keepdims=True)
    ) / own_length
    out_cross = forward_homes(out_final, out_homes[1])

    wait(*small_spread)
    small = []
    for tile in range(SMALL_TILES):
        both = small_slots[tile // 2, tile % 2]
        small += [both[0:8], both[8:16]]
    probe_out[...] = jnp.sum(jnp.concatenate(small[9:], axis=1)[:, :ROWS], axis=0, keepdims=True)
    patch_sum = jnp.concatenate(small[:9], axis=1) * (1.0 / math.sqrt(HEAD_DIM))
    probe_columns = probe.T
    for pair in range(4):
        parts = []
        for head in (2 * pair, 2 * pair + 1):
            column = probe_columns[head * HEAD_DIM : head * HEAD_DIM + HEAD_DIM, head : head + 1]
            parts.append(column * patch_sum[head : head + 1])
        key_out[pair * 144 : pair * 144 + 144, :] = jnp.concatenate(parts, axis=0).astype(bf16)
    value_cross = forward_homes(value_final, value_homes[1])

    unpack(out_final, core, out_out)
    wait(out_final.at[1 - core], out_cross)
    unpack(out_final, 1 - core, out_out)
    unpack(value_final, core, value_out)
    wait(value_final.at[1 - core], value_cross)
    unpack(value_final, 1 - core, value_out)
    for end in ends:
        wait(*end)


def finish_kernel(*refs):
    count = len(refs) // 2
    sources, targets, sem = refs[:count], refs[count : 2 * count], refs[2 * count]
    copies = [
        pltpu.make_async_copy(source, target, sem.at[slot])
        for slot, (source, target) in enumerate(zip(sources, targets))
    ]
    for copy in copies:
        copy.start()
    for copy in copies:
        copy.wait()


def in_hbm(array):
    return pltpu.with_memory_space_constraint(array, pltpu.HBM)


def on_device(
    patches, captions, probe_query, key_weight, value_weight, out_weight, logit_scale, logit_bias
):
    f32, bf16 = jnp.float32, jnp.bfloat16
    vmem = pl.BlockSpec(memory_space=pltpu.VMEM)
    smem = pl.BlockSpec(memory_space=pltpu.SMEM)
    hbm = pl.BlockSpec(memory_space=pltpu.HBM)
    dma = pltpu.SemaphoreType.DMA
    shapes = (
        jax.ShapeDtypeStruct((IMG_DEV, D), f32),
        jax.ShapeDtypeStruct((1, ROWS), f32),
        jax.ShapeDtypeStruct((ROWS, D), bf16),
        jax.ShapeDtypeStruct((ROWS, D), bf16),
        jax.ShapeDtypeStruct((ROWS, D), bf16),
    )
    results = pl.pallas_call(
        whole_kernel,
        out_shape=shapes,
        in_specs=[smem, smem, hbm, hbm, hbm, hbm, hbm, hbm],
        out_specs=[vmem] * 5,
        scratch_shapes=[
            pltpu.VMEM((FLAT, D), bf16),
            pltpu.VMEM((IMG_DEV, D), bf16),
            pltpu.VMEM((ROWS,), bf16),
            pltpu.VMEM((VALUE_AT + ROWS, D), bf16),
            pltpu.VMEM((ROWS, D), bf16),
            pltpu.VMEM((FLAT, ROWS), bf16),
            pltpu.VMEM((FLAT, ROWS), bf16),
            pltpu.VMEM((64, PATCHES), f32),
            pltpu.VMEM((64, PATCHES), f32),
            pltpu.VMEM((3, 8, D), f32),
            pltpu.VMEM((3, 8, D), f32),
            pltpu.VMEM((2, 8, D), f32),
            pltpu.VMEM((ROWS, 8), f32),
            pltpu.VMEM((16, D), f32),
            pltpu.VMEM((16, D), bf16),
            pltpu.VMEM((HALF_ROWS + 16, FLAT), bf16),
            pltpu.VMEM((HALF_ROWS, FLAT), bf16),
            pltpu.VMEM((16, FLAT), bf16),
            pltpu.VMEM((8, WIDE), f32),
            pltpu.VMEM((LIST, 16, 128), bf16),
            pltpu.VMEM((LIST, 16, 128), bf16),
            pltpu.VMEM((LIST, 16, 128), f32),
            pltpu.VMEM((4, 2, 16, D), bf16),
            pltpu.VMEM((16, D), bf16),
            pltpu.VMEM((8, WIDE), f32),
            pltpu.VMEM((8, WIDE), f32),
            pltpu.VMEM((3, 8, WIDE), f32),
            pltpu.VMEM((ROWS, 64), f32),
            pltpu.VMEM((LIST, 16, 128), f32),
            pltpu.VMEM((12, PIECE, 16, 128), bf16),
            pltpu.VMEM((12, PIECE, 16, 128), bf16),
            pltpu.VMEM((4, SLOTS, 16, 128), f32),
            pltpu.VMEM((3, SLOTS, 16, 128), f32),
            pltpu.VMEM((16, 16, 128), f32),
            pltpu.VMEM((7, OWNED, 16, 128), f32),
            pltpu.VMEM((OWNED, 16, 128), bf16),
            pltpu.VMEM((16, 16, 128), bf16),
            pltpu.VMEM((OWNED, 16, 128), f32),
            pltpu.VMEM((4, OWNED, 16, 128), f32),
            pltpu.VMEM((2, 4, 4, PIECE, 16, 128), bf16),
            pltpu.VMEM((4, PIECE, 16, 128), f32),
            pltpu.VMEM((3, PIECE, 16, 128), f32),
            pltpu.VMEM((16, 16, 128), f32),
            pltpu.VMEM((7, OWNED, 16, 128), f32),
            pltpu.VMEM((OWNED, 16, 128), bf16),
            pltpu.VMEM((16, 16, 128), bf16),
            pltpu.VMEM((2, 4, 4, PIECE, 16, 128), bf16),
            dma((9,)),
            dma((58,)),
        ],
        compiler_params=pltpu.CompilerParams(
            collective_id=0, has_side_effects=True, vmem_limit_bytes=40 * 1024 * 1024
        ),
        name="whole",
    )(
        logit_scale,
        logit_bias,
        in_hbm(patches.reshape(FLAT, D)),
        in_hbm(captions),
        in_hbm(probe_query),
        in_hbm(key_weight.T),
        in_hbm(value_weight.T),
        in_hbm(out_weight),
    )
    caption_grad, probe_grad, key_turned, value_turned, out_grad = pl.pallas_call(
        finish_kernel,
        out_shape=shapes,
        in_specs=[vmem] * 5,
        out_specs=[hbm] * 5,
        scratch_shapes=[dma((5,))],
        compiler_params=pltpu.CompilerParams(vmem_limit_bytes=8 * 1024 * 1024),
        name="finish",
    )(*results)
    return (caption_grad, probe_grad.reshape(ROWS), key_turned.T, value_turned.T, out_grad)


def solution(mesh):
    placed = (P("dp", None, None), P("dp", None), P(), P(), P(), P(), P(), P())
    return jax.shard_map(
        on_device,
        mesh=mesh,
        in_specs=placed,
        out_specs=(P("dp", None), P(), P(), P(), P()),
        check_vma=False,
    )
```

time: 75.1 us -> 72.8 us (0.969)
  Pallas kernels: 72.5 us -> 70.2 us
    pallas_call x2, Pallas kernels: 72.5 us -> 70.2 us  [the longest x1 68.2 us: on_device(): pl.pallas_call(whole_kernel, out_shape=shapes, in_specs=[smem, smem, hbm,...]
where the time goes in v4:
time: 72.8 us; the launch traced here: 72.7 us
  Pallas kernels  70.2 us (96%)
  between operations  1.94 us (3%)
    pallas_call x1, Pallas kernels, on_device(): pl.pallas_call(whole_kernel, out_shape=shapes, in_specs=[smem, smem, hbm,...  68.2 us
    pallas_call x1, Pallas kernels, on_device(): pl.pallas_call(finish_kernel, out_shape=shapes, in_specs=[vmem] * 5, out_...  1.99 us

profile of v4, /device:TPU:1, one launch (start us, length us, event | category | flops | bytes accessed | tf_op | source)
XLA Modules:
  0.0 72.7 jit_solution(18419370597615960449)
XLA Ops:
  1.9 68.2 %whole.1 = (f32[8,1152]{1,0:T(8,128)S(1)}, f32[1,576]{1,0:T(1,128)S(1)}, bf16[576,1152]{1,0:T(8,128)(2,1)S(1)}, bf16[576,1152]{1,0:T(8,128)(2,1)S(1)}, bf16[576,1152]{1,0:T(8,128)(2,1)S(1)}) custom-call(f32[1]{0:T(128)S(6)} %copy.13.scale_ref, f32[1]{0:T(128)S(6)} %copy.14.bias_ref, bf16[2048,1152]{1,0:T(8,128)(2,1)} %bitcast.5, ...), custom_call_target="tpu_custom_call" | custom-call | tf_op jit(solution)/shard_map/whole/pallas_call | solution.py:596
  70.1 2.0 %finish.1 = (f32[8,1152]{1,0:T(8,128)}, f32[1,576]{1,0:T(1,128)S(1)}, bf16[576,1152]{1,0:T(8,128)(2,1)}, bf16[576,1152]{1,0:T(8,128)(2,1)}, bf16[576,1152]{1,0:T(8,128)(2,1)}) custom-call(f32[8,1152]{1,0:T(8,128)S(1)} %get-tuple-element.15.refs_0_, f32[1,576]{1,0:T(1,128)S(1)} %get-tuple-element.16.refs_1_, bf16[576,1152]{1,0:T(8,128)(2,1)S(1)} %get-tuple-element.17.refs_2_, ...), custom_call_target="tpu_custom_call" | custom-call | tf_op jit(solution)/shard_map/finish/pallas_call | solution.py:666
  72.1 0.6 reduce

commit v5 on v4

--- a/solution.py
+++ b/solution.py
@@ -27,7 +27,7 @@
 OWNERS = 6
 SLOTS = 14
 SMALL_AT = 12
-WIDE = 1792
+WIDE = 1280
 SMALL_TILES = WIDE // 256
 
 norm_epsilon = 1e-06
@@ -116,6 +116,7 @@
     out_grid,
     out_second,
     out_total,
+    out_leaving,
     out_third,
     out_owned,
     out_all,
@@ -222,7 +223,7 @@
 
     load(key_ref, weights.at[0:ROWS], 4).wait()
     load(value_ref, weights.at[VALUE_AT : VALUE_AT + ROWS], 5).wait()
-    lax.fori_loop(0, 3, project, 0)
+    lax.fori_loop(0, 2, project, 0)
     load(captions_ref, captions, 7).wait()
     own_unit, own_length = normalize(captions[...].astype(f32))
     units[0] = own_unit
@@ -230,7 +231,7 @@
     unit_copies = send_all(
         [((me + step) % 256, units.at[0], units.at[step]) for step in (1, 2)], units.at[1:3]
     )
-    lax.fori_loop(3, 4, project, 0)
+    lax.fori_loop(2, 4, project, 0)
 
     score = scores[...] * (1.0 / math.sqrt(HEAD_DIM))
     raised = jnp.exp(score - jnp.max(score, axis=-1, keepdims=True))
@@ -285,14 +286,6 @@
         attention_grad - jnp.sum(attend * attention_grad, axis=-1, keepdims=True)
     )
 
-    wait(*rows_copy)
-    rows_all[0, 0] = rows_own[...]
-    rows_all[0, 1] = rows_got[...]
-    row_gathers = send_all(
-        [(first_peer(step)[0], rows_all.at[0], rows_all.at[step]) for step in (2, 1, 3)],
-        rows_all.at[1:4],
-    )
-
     def value_rows_grad(start, target):
         for image in range(IMG_DEV):
             for pair in range(2):
@@ -313,6 +306,14 @@
             [part, jnp.zeros((8, PATCHES), f32)], axis=0
         ).astype(bf16)
         score_rows[:, lanes] = split_low(part)
+
+    wait(*rows_copy)
+    rows_all[0, 0] = rows_own[...]
+    rows_all[0, 1] = rows_got[...]
+    row_gathers = send_all(
+        [(first_peer(step)[0], rows_all.at[0], rows_all.at[step]) for step in (2, 1, 3)],
+        rows_all.at[1:4],
+    )
 
     value_send[HALF:] = jnp.zeros((LIST - HALF, 16, 128), bf16)
     pair_leave, pair_arrive = new_sem(), new_sem()
@@ -329,9 +330,12 @@
             part = slice(start, start + PART if block < 4 else LIST)
             send(other, value_send.at[part], value_got.at[part], pair_leave, pair_arrive)
     probe_part = dot(score_rows[...], keys[...])
-    probe_part = jnp.where(own_head, probe_part[0:8] + probe_part[8:16], 0.0) * (1.0 / math.sqrt(HEAD_DIM))
+    probe_part = jnp.where(own_head, probe_part[0:8] + probe_part[8:16], 0.0)
+    probe_part = jnp.sum(probe_part, axis=0, keepdims=True) * (1.0 / math.sqrt(HEAD_DIM))
     small_own[:, D:WIDE] = jnp.zeros((8, WIDE - D), f32)
-    small_own[:, D : D + ROWS] = probe_part
+    for row in range(5):
+        count = min(128, ROWS - row * 128)
+        small_own[row : row + 1, D : D + count] = probe_part[:, row * 128 : row * 128 + count]
     small_copy = send_all([(other, small_own, small_got)], small_got)
 
     value_rows_grad(core * 4, home_rows)
@@ -343,11 +347,6 @@
             value_own[tile] = term[row : row + 16, lane : lane + 128]
     value_own[HALF:] = jnp.zeros((LIST - HALF, 16, 128), f32)
 
-    wait(*small_copy)
-    small_pair[...] = small_own[...] + small_got[...]
-    small_gathers = send_all(
-        [(first_peer(step)[0], small_pair, small_all.at[step - 1]) for step in (2, 1, 3)], small_all
-    )
     def piece_at(place, piece):
         return pl.ds(place * PART + piece * PIECE, PIECE)
 
@@ -364,6 +363,11 @@
             copies.append((device, first_send.at[slot], first_got.at[slot]))
         first_copies.append((ahead, send_all(copies, first_got.at[ahead * 3 : ahead * 3 + 3])))
 
+    wait(*small_copy)
+    small_pair[...] = small_own[...] + small_got[...]
+    small_gathers = send_all(
+        [(first_peer(step)[0], small_pair, small_all.at[step - 1]) for step in (2, 1, 3)], small_all
+    )
     wait(*row_gathers)
     rows = rows_all[...].astype(f32).reshape(8, 16, D)
     embedding_grads = rows[:, :8].reshape(64, D).astype(bf16)
@@ -379,7 +383,7 @@
     out_own[HALF:] = jnp.zeros((LIST - HALF, 16, 128), f32)
 
     for piece in range(4):
-        out_grid[piece] = out_own[piece_at(first, piece)]
+        out_grid[piece] = out_own[piece_at(first, piece)].astype(bf16)
     out_copies = send_all(
         [
             (second_peer(step)[0], out_grid.at[second_peer(step)[1]], out_second.at[step - 1])
@@ -411,29 +415,47 @@
     def z_order():
         return (4, 3, 5, 2, 6, 1, 7)
 
-    def send_third(total, got):
-        copies = []
+    def send_third(total, got, owners):
+        leave, arrive = new_sem(), new_sem()
         for step in z_order():
             device, place = third_peer(step)
-            copies.append((device, total.at[pl.ds(place * OWNED, OWNED)], got.at[step - 1]))
-        return send_all(copies, got)
-
-    def send_back(total, got, copies, owned, every):
-        wait(*copies)
+
+            @pl.when(place < owners)
+            def _():
+                source = total.at[pl.ds(place * OWNED, OWNED)]
+                send(device, source, got.at[step - 1], leave, arrive)
+
+        return leave, arrive
+
+    def send_back(total, got, leave, arrive, owners, owned, every):
+        @pl.when(z < owners)
+        def _():
+            wait(got, arrive)
+            wait(got.at[0 : owners - 1], leave)
+
+        @pl.when(z >= owners)
+        def _():
+            wait(got.at[0:owners], leave)
+
+        leave, arrive = new_sem(), new_sem()
         mine = pl.ds(z * OWNED, OWNED)
-        result = total[mine]
-        for slot in range(7):
-            result = result + got[slot]
-        owned[...] = result.astype(bf16)
-        every[mine] = result.astype(bf16)
-        leave, arrive = new_sem(), new_sem()
+
+        @pl.when(z < owners)
+        def _():
+            result = total[mine]
+            for slot in range(7):
+                result = result + got[slot].astype(f32)
+            total[mine] = result
 
         @pl.when(z < OWNERS)
         def _():
+            result = total[mine].astype(bf16)
+            owned[...] = result
+            every[mine] = result
             for step in z_order():
                 send(third_peer(step)[0], owned, every.at[mine], leave, arrive)
 
-        return result, leave, arrive
+        return leave, arrive
 
     def end_back(every, leave, arrive):
         @pl.when(z < OWNERS)
@@ -486,24 +508,31 @@
             target[row, lane : lane + 128] = final[which, place, at // PIECE, at % PIECE]
 
     wait(*out_copies)
-    out_total[0:PIECE] = out_grid[second] + out_second[0] + out_second[1] + out_second[2]
+    out_sum = out_own[piece_at(first, second)]
+    for slot in range(3):
+        out_sum = out_sum + out_second[slot].astype(f32)
+    out_total[0:PIECE] = out_sum
     out_total[PIECE:] = jnp.zeros((16 - PIECE, 16, 128), f32)
-    out_thirds = send_third(out_total, out_third)
+    out_leaving[...] = out_total[...].astype(bf16)
+    out_thirds = send_third(out_leaving, out_third, OWNERS)
 
     wait(value_second, value_arrive)
     value_total[0:SLOTS] = value_grid[second] + value_second[0] + value_second[1] + value_second[2]
     value_total[SLOTS:] = jnp.zeros((16 - SLOTS, 16, 128), f32)
-    value_thirds = send_third(value_total, value_third)
-
-    _, *out_back = send_back(out_total, out_third, out_thirds, out_owned, out_all)
-
-    small_sum, *value_back = send_back(value_total, value_third, value_thirds, value_owned, value_all)
-    small_owned[...] = small_sum
+    value_thirds = send_third(value_total, value_third, OWNERS + 1)
+
+    out_back = send_back(out_total, out_third, *out_thirds, OWNERS, out_owned, out_all)
+
+    value_back = send_back(
+        value_total, value_third, *value_thirds, OWNERS + 1, value_owned, value_all
+    )
     mine = small_slots.at[second]
     small_leave, small_arrive = new_sem(), new_sem()
 
     @pl.when(z == OWNERS)
     def _():
+        small_sum = value_total[OWNERS * OWNED : (OWNERS + 1) * OWNED]
+        small_owned[...] = small_sum
         small_slots[second] = small_sum
         for step in z_order():
             send(third_peer(step)[0], small_owned, mine, small_leave, small_arrive)
@@ -513,10 +542,11 @@
 
     end_back(value_all, *value_back)
     value_spread, *value_homes = send_spread(value_all, value_final)
+    forward_spread(out_final, out_spread, *out_homes)
 
     @pl.when(z == OWNERS)
     def _():
-        wait(value_total.at[0 : 7 * OWNED], small_leave)
+        wait(value_third, small_leave)
 
     @pl.when(z != OWNERS)
     def _():
@@ -525,7 +555,6 @@
     small_spread = send_all(
         [(second_peer(step)[0], mine, mine) for step in (2, 1, 3)], small_slots.at[0:3]
     )
-    forward_spread(out_final, out_spread, *out_homes)
     forward_spread(value_final, value_spread, *value_homes)
 
     wait(*visit_copies)
@@ -540,7 +569,8 @@
     for tile in range(SMALL_TILES):
         both = small_slots[tile // 2, tile % 2]
         small += [both[0:8], both[8:16]]
-    probe_out[...] = jnp.sum(jnp.concatenate(small[9:], axis=1)[:, :ROWS], axis=0, keepdims=True)
+    probe_sum = jnp.concatenate([small[9][row : row + 1] for row in range(5)], axis=1)
+    probe_out[...] = jnp.sum(probe_sum[:, :ROWS], axis=0)
     patch_sum = jnp.concatenate(small[:9], axis=1) * (1.0 / math.sqrt(HEAD_DIM))
     probe_columns = probe.T
     for pair in range(4):
@@ -588,7 +618,7 @@
     dma = pltpu.SemaphoreType.DMA
     shapes = (
         jax.ShapeDtypeStruct((IMG_DEV, D), f32),
-        jax.ShapeDtypeStruct((1, ROWS), f32),
+        jax.ShapeDtypeStruct((ROWS,), f32),
         jax.ShapeDtypeStruct((ROWS, D), bf16),
         jax.ShapeDtypeStruct((ROWS, D), bf16),
         jax.ShapeDtypeStruct((ROWS, D), bf16),
@@ -639,10 +669,11 @@
             pltpu.VMEM((OWNED, 16, 128), f32),
             pltpu.VMEM((4, OWNED, 16, 128), f32),
             pltpu.VMEM((2, 4, 4, PIECE, 16, 128), bf16),
-            pltpu.VMEM((4, PIECE, 16, 128), f32),
-            pltpu.VMEM((3, PIECE, 16, 128), f32),
+            pltpu.VMEM((4, PIECE, 16, 128), bf16),
+            pltpu.VMEM((3, PIECE, 16, 128), bf16),
             pltpu.VMEM((16, 16, 128), f32),
-            pltpu.VMEM((7, OWNED, 16, 128), f32),
+            pltpu.VMEM((16, 16, 128), bf16),
+            pltpu.VMEM((7, OWNED, 16, 128), bf16),
             pltpu.VMEM((OWNED, 16, 128), bf16),
             pltpu.VMEM((16, 16, 128), bf16),
             pltpu.VMEM((2, 4, 4, PIECE, 16, 128), bf16),
@@ -672,7 +703,7 @@
         compiler_params=pltpu.CompilerParams(vmem_limit_bytes=8 * 1024 * 1024),
         name="finish",
     )(*results)
-    return (caption_grad, probe_grad.reshape(ROWS), key_turned.T, value_turned.T, out_grad)
+    return (caption_grad, probe_grad, key_turned.T, value_turned.T, out_grad)
 
 
 def solution(mesh):

time: 72.8 us -> 69.9 us (0.960)
  Pallas kernels: 70.2 us -> 67.9 us
    pallas_call x1, Pallas kernels: 68.2 us -> 65.9 us  [on_device(): pl.pallas_call(whole_kernel, out_shape=shapes, in_specs=[smem, smem, hbm,...]
where the time goes in v5:
time: 69.9 us; the launch traced here: 69.8 us
  Pallas kernels  67.9 us (97%)
  between operations  1.93 us (3%)
    pallas_call x1, Pallas kernels, on_device(): pl.pallas_call(whole_kernel, out_shape=shapes, in_specs=[smem, smem, hbm,...  65.9 us
    pallas_call x1, Pallas kernels, on_device(): pl.pallas_call(finish_kernel, out_shape=shapes, in_specs=[vmem] * 5, out_...  2 us

profile of v5, /device:TPU:1, one launch (start us, length us, event | category | flops | bytes accessed | tf_op | source)
XLA Modules:
  0.0 69.8 jit_solution(13527022872348188183)
XLA Ops:
  1.9 65.9 %whole.1 = (f32[8,1152]{1,0:T(8,128)S(1)}, f32[576]{0:T(1024)S(1)}, bf16[576,1152]{1,0:T(8,128)(2,1)S(1)}, bf16[576,1152]{1,0:T(8,128)(2,1)S(1)}, bf16[576,1152]{1,0:T(8,128)(2,1)S(1)}) custom-call(f32[1]{0:T(128)S(6)} %copy.13.scale_ref, f32[1]{0:T(128)S(6)} %copy.14.bias_ref, bf16[2048,1152]{1,0:T(8,128)(2,1)} %bitcast.5, bf16[8,1152]{1,0:T(8,128)(2,1)} %captions_ref.1, ...), custom_call_target="tpu_custom_call" | custom-call | tf_op jit(solution)/shard_map/whole/pallas_call | solution.py:626
  67.8 2.0 %finish.1 = (f32[8,1152]{1,0:T(8,128)}, f32[576]{0:T(1024)}, bf16[576,1152]{1,0:T(8,128)(2,1)}, bf16[576,1152]{1,0:T(8,128)(2,1)}, bf16[576,1152]{1,0:T(8,128)(2,1)}) custom-call(f32[8,1152]{1,0:T(8,128)S(1)} %get-tuple-element.15.refs_0_, f32[576]{0:T(1024)S(1)} %get-tuple-element.16.refs_1_, bf16[576,1152]{1,0:T(8,128)(2,1)S(1)} %get-tuple-element.17.refs_2_, ...), custom_call_target="tpu_custom_call" | custom-call | tf_op jit(solution)/shard_map/finish/pallas_call | solution.py:697

commit v6 on v5

--- a/solution.py
+++ b/solution.py
@@ -25,7 +25,6 @@
 LIST = 168
 OWNED = 2
 OWNERS = 6
-SLOTS = 14
 SMALL_AT = 12
 WIDE = 1280
 SMALL_TILES = WIDE // 256
@@ -106,6 +105,8 @@
     first_got,
     value_grid,
     value_second,
+    small_grid,
+    small_second,
     value_total,
     value_third,
     value_owned,
@@ -315,7 +316,7 @@
         rows_all.at[1:4],
     )
 
-    value_send[HALF:] = jnp.zeros((LIST - HALF, 16, 128), bf16)
+    value_send[HALF:] = jnp.zeros((LIST - HALF, 16, 128), f32)
     pair_leave, pair_arrive = new_sem(), new_sem()
     ends.append((value_send, pair_leave))
     for block in range(5):
@@ -323,7 +324,7 @@
         term = dot(away_rows[...], x_all[:, lanes])
         for tile in range(block * 36, min(block * 36 + 36, HALF)):
             row, lane = tile % 18 * 16, tile // 18 * 128 - block * 256
-            value_send[tile] = term[row : row + 16, lane : lane + 128].astype(bf16)
+            value_send[tile] = term[row : row + 16, lane : lane + 128]
         small_own[:, lanes] = term[HALF_ROWS : HALF_ROWS + 8]
         if block > 0:
             start = (block - 1) * PART
@@ -359,7 +360,7 @@
             device, place = first_peer(step)
             slot = ahead * 3 + step - 1
             part = piece_at(place, piece)
-            first_send[slot] = (value_own[part] + value_got[part].astype(f32)).astype(bf16)
+            first_send[slot] = (value_own[part] + value_got[part]).astype(bf16)
             copies.append((device, first_send.at[slot], first_got.at[slot]))
         first_copies.append((ahead, send_all(copies, first_got.at[ahead * 3 : ahead * 3 + 3])))
 
@@ -392,25 +393,33 @@
         out_second,
     )
 
-    wait(*small_gathers)
-    small = small_pair[...] + small_all[0] + small_all[1] + small_all[2]
-    value_grid[:, PIECE:] = jnp.zeros((4, SLOTS - PIECE, 16, 128), f32)
-    for tile in range(SMALL_TILES):
-        at = (tile // 2, SMALL_AT + tile % 2)
-        value_grid[at[0], at[1], 0:8] = small[:, tile * 256 : tile * 256 + 128]
-        value_grid[at[0], at[1], 8:16] = small[:, tile * 256 + 128 : tile * 256 + 256]
     value_leave, value_arrive = new_sem(), new_sem()
     for ahead, copies in first_copies:
         wait(*copies)
         device, piece = second_peer(ahead)
         part = piece_at(first, piece)
-        term = value_own[part] + value_got[part].astype(f32)
+        term = value_own[part] + value_got[part]
         for step in (1, 2, 3):
             term = term + first_got[ahead * 3 + step - 1].astype(f32)
-        value_grid[piece, 0:PIECE] = term
-        if ahead > 0:
+        if ahead == 0:
+            value_total[0:PIECE] = term
+        else:
+            value_grid[piece] = term.astype(bf16)
             send(device, value_grid.at[piece], value_second.at[ahead - 1], value_leave, value_arrive)
     ends.append((value_second, value_leave))
+    wait(*small_gathers)
+    small = small_pair[...] + small_all[0] + small_all[1] + small_all[2]
+    small_grid[...] = jnp.zeros((4, OWNED, 16, 128), f32)
+    for tile in range(SMALL_TILES):
+        small_grid[tile // 2, tile % 2, 0:8] = small[:, tile * 256 : tile * 256 + 128]
+        small_grid[tile // 2, tile % 2, 8:16] = small[:, tile * 256 + 128 : tile * 256 + 256]
+    small_copies = send_all(
+        [
+            (second_peer(step)[0], small_grid.at[second_peer(step)[1]], small_second.at[step - 1])
+            for step in (2, 1, 3)
+        ],
+        small_second,
+    )
 
     def z_order():
         return (4, 3, 5, 2, 6, 1, 7)
@@ -517,8 +526,15 @@
     out_thirds = send_third(out_leaving, out_third, OWNERS)
 
     wait(value_second, value_arrive)
-    value_total[0:SLOTS] = value_grid[second] + value_second[0] + value_second[1] + value_second[2]
-    value_total[SLOTS:] = jnp.zeros((16 - SLOTS, 16, 128), f32)
+    value_sum = value_total[0:PIECE]
+    for slot in range(3):
+        value_sum = value_sum + value_second[slot].astype(f32)
+    value_total[0:PIECE] = value_sum
+    wait(*small_copies)
+    value_total[PIECE:] = jnp.zeros((16 - PIECE, 16, 128), f32)
+    value_total[SMALL_AT : SMALL_AT + OWNED] = (
+        small_grid[second] + small_second[0] + small_second[1] + small_second[2]
+    )
     value_thirds = send_third(value_total, value_third, OWNERS + 1)
 
     out_back = send_back(out_total, out_third, *out_thirds, OWNERS, out_owned, out_all)
@@ -648,8 +664,8 @@
             pltpu.VMEM((HALF_ROWS, FLAT), bf16),
             pltpu.VMEM((16, FLAT), bf16),
             pltpu.VMEM((8, WIDE), f32),
-            pltpu.VMEM((LIST, 16, 128), bf16),
-            pltpu.VMEM((LIST, 16, 128), bf16),
+            pltpu.VMEM((LIST, 16, 128), f32),
+            pltpu.VMEM((LIST, 16, 128), f32),
             pltpu.VMEM((LIST, 16, 128), f32),
             pltpu.VMEM((4, 2, 16, D), bf16),
             pltpu.VMEM((16, D), bf16),
@@ -660,8 +676,10 @@
             pltpu.VMEM((LIST, 16, 128), f32),
             pltpu.VMEM((12, PIECE, 16, 128), bf16),
             pltpu.VMEM((12, PIECE, 16, 128), bf16),
-            pltpu.VMEM((4, SLOTS, 16, 128), f32),
-            pltpu.VMEM((3, SLOTS, 16, 128), f32),
+            pltpu.VMEM((4, PIECE, 16, 128), bf16),
+            pltpu.VMEM((3, PIECE, 16, 128), bf16),
+            pltpu.VMEM((4, OWNED, 16, 128), f32),
+            pltpu.VMEM((3, OWNED, 16, 128), f32),
             pltpu.VMEM((16, 16, 128), f32),
             pltpu.VMEM((7, OWNED, 16, 128), f32),
             pltpu.VMEM((OWNED, 16, 128), bf16),
@@ -678,7 +696,7 @@
             pltpu.VMEM((16, 16, 128), bf16),
             pltpu.VMEM((2, 4, 4, PIECE, 16, 128), bf16),
             dma((9,)),
-            dma((58,)),
+            dma((60,)),
         ],
         compiler_params=pltpu.CompilerParams(
             collective_id=0, has_side_effects=True, vmem_limit_bytes=40 * 1024 * 1024

time: 69.9 us -> 68.2 us (0.976)
  Pallas kernels: 67.9 us -> 66.2 us
    pallas_call x1, Pallas kernels: 65.9 us -> 64.2 us  [on_device(): pl.pallas_call(whole_kernel, out_shape=shapes, in_specs=[smem, smem, hbm,...]
where the time goes in v6:
time: 68.2 us; the launch traced here: 68.1 us
  Pallas kernels  66.2 us (97%)
  between operations  1.93 us (3%)
    pallas_call x1, Pallas kernels, on_device(): pl.pallas_call(whole_kernel, out_shape=shapes, in_specs=[smem, smem, hbm,...  64.2 us
    pallas_call x1, Pallas kernels, on_device(): pl.pallas_call(finish_kernel, out_shape=shapes, in_specs=[vmem] * 5, out_...  2 us

profile of v6, /device:TPU:1, one launch (start us, length us, event | category | flops | bytes accessed | tf_op | source)
XLA Modules:
  0.0 68.1 jit_solution(13107314452123112722)
XLA Ops:
  1.9 64.2 %whole.1 = (f32[8,1152]{1,0:T(8,128)S(1)}, f32[576]{0:T(1024)S(1)}, bf16[576,1152]{1,0:T(8,128)(2,1)S(1)}, bf16[576,1152]{1,0:T(8,128)(2,1)S(1)}, bf16[576,1152]{1,0:T(8,128)(2,1)S(1)}) custom-call(f32[1]{0:T(128)S(6)} %copy.13.scale_ref, f32[1]{0:T(128)S(6)} %copy.14.bias_ref, bf16[2048,1152]{1,0:T(8,128)(2,1)} %bitcast.5, bf16[8,1152]{1,0:T(8,128)(2,1)} %captions_ref.1, ...), custom_call_target="tpu_custom_call" | custom-call | tf_op jit(solution)/shard_map/whole/pallas_call | solution.py:642
  66.1 2.0 %finish.1 = (f32[8,1152]{1,0:T(8,128)}, f32[576]{0:T(1024)}, bf16[576,1152]{1,0:T(8,128)(2,1)}, bf16[576,1152]{1,0:T(8,128)(2,1)}, bf16[576,1152]{1,0:T(8,128)(2,1)}) custom-call(f32[8,1152]{1,0:T(8,128)S(1)} %get-tuple-element.15.refs_0_, f32[576]{0:T(1024)S(1)} %get-tuple-element.16.refs_1_, bf16[576,1152]{1,0:T(8,128)(2,1)S(1)} %get-tuple-element.17.refs_2_, ...), custom_call_target="tpu_custom_call" | custom-call | tf_op jit(solution)/shard_map/finish/pallas_call | solution.py:715

commit v7 on v6

--- a/solution.py
+++ b/solution.py
@@ -308,14 +308,6 @@
         ).astype(bf16)
         score_rows[:, lanes] = split_low(part)
 
-    wait(*rows_copy)
-    rows_all[0, 0] = rows_own[...]
-    rows_all[0, 1] = rows_got[...]
-    row_gathers = send_all(
-        [(first_peer(step)[0], rows_all.at[0], rows_all.at[step]) for step in (2, 1, 3)],
-        rows_all.at[1:4],
-    )
-
     value_send[HALF:] = jnp.zeros((LIST - HALF, 16, 128), f32)
     pair_leave, pair_arrive = new_sem(), new_sem()
     ends.append((value_send, pair_leave))
@@ -326,6 +318,14 @@
             row, lane = tile % 18 * 16, tile // 18 * 128 - block * 256
             value_send[tile] = term[row : row + 16, lane : lane + 128]
         small_own[:, lanes] = term[HALF_ROWS : HALF_ROWS + 8]
+        if block == 0:
+            wait(*rows_copy)
+            rows_all[0, 0] = rows_own[...]
+            rows_all[0, 1] = rows_got[...]
+            row_gathers = send_all(
+                [(first_peer(step)[0], rows_all.at[0], rows_all.at[step]) for step in (2, 1, 3)],
+                rows_all.at[1:4],
+            )
         if block > 0:
             start = (block - 1) * PART
             part = slice(start, start + PART if block < 4 else LIST)

time: 68.2 us -> 68.1 us (level)
  no operation moved by 1% of the time
where the time goes in v7:
time: 68.1 us; the launch traced here: 68 us
  Pallas kernels  66 us (97%)
  between operations  1.93 us (3%)
    pallas_call x1, Pallas kernels, on_device(): pl.pallas_call(whole_kernel, out_shape=shapes, in_specs=[smem, smem, hbm,...  64 us
    pallas_call x1, Pallas kernels, on_device(): pl.pallas_call(finish_kernel, out_shape=shapes, in_specs=[vmem] * 5, out_...  2 us

profile of v7, /device:TPU:1, one launch (start us, length us, event | category | flops | bytes accessed | tf_op | source)
XLA Modules:
  0.0 68.0 jit_solution(8080825016502378812)
XLA Ops:
  1.9 64.0 %whole.1 = (f32[8,1152]{1,0:T(8,128)S(1)}, f32[576]{0:T(1024)S(1)}, bf16[576,1152]{1,0:T(8,128)(2,1)S(1)}, bf16[576,1152]{1,0:T(8,128)(2,1)S(1)}, bf16[576,1152]{1,0:T(8,128)(2,1)S(1)}) custom-call(f32[1]{0:T(128)S(6)} %copy.13.scale_ref, f32[1]{0:T(128)S(6)} %copy.14.bias_ref, bf16[2048,1152]{1,0:T(8,128)(2,1)} %bitcast.5, bf16[8,1152]{1,0:T(8,128)(2,1)} %captions_ref.1, ...), custom_call_target="tpu_custom_call" | custom-call | tf_op jit(solution)/shard_map/whole/pallas_call | solution.py:642
  66.0 2.0 %finish.1 = (f32[8,1152]{1,0:T(8,128)}, f32[576]{0:T(1024)}, bf16[576,1152]{1,0:T(8,128)(2,1)}, bf16[576,1152]{1,0:T(8,128)(2,1)}, bf16[576,1152]{1,0:T(8,128)(2,1)}) custom-call(f32[8,1152]{1,0:T(8,128)S(1)} %get-tuple-element.15.refs_0_, f32[576]{0:T(1024)S(1)} %get-tuple-element.16.refs_1_, bf16[576,1152]{1,0:T(8,128)(2,1)S(1)} %get-tuple-element.17.refs_2_, ...), custom_call_target="tpu_custom_call" | custom-call | tf_op jit(solution)/shard_map/finish/pallas_call | solution.py:715
